TPU v7x, 32 devices: a whole 2x2x4 slice. The times are simulated.
32 devices in a mesh: rows: 8 (over z, y), seq: 4 (over x, core).
Axes of the slice: x: 2, y: 2, z: 4, core: 2. Of those that a mesh axis runs over, the one named last changes fastest.
Arguments:
- tokens: bfloat16 [16, 2048, 768], P('rows', 'seq'), may hold values from -6 to 6
- segments: int32 [16, 2048], P('rows'), may hold values from 0 to 1022, as said below
- query_weight: bfloat16 [768, 768], replicated, may hold values from -0.21875 to 0.21875
- query_bias: float32 [768], replicated, may hold values from -1.75 to 1.75
- key_weight: bfloat16 [768, 768], replicated, may hold values from -0.21875 to 0.21875
- value_weight: bfloat16 [768, 768], replicated, may hold values from -0.21875 to 0.21875
- value_bias: float32 [768], replicated, may hold values from -1.75 to 1.75
- out_weight: bfloat16 [768, 768], replicated, may hold values from -0.875 to 0.875
- out_bias: float32 [768], replicated, may hold values from -1.75 to 1.75
- first_gain: float32 [768], replicated, may hold values from 0.5 to 1.5
- first_shift: float32 [768], replicated, may hold values from -1.75 to 1.75
- up_weight: bfloat16 [768, 3072], replicated, may hold values from -0.21875 to 0.21875
- up_bias: float32 [3072], replicated, may hold values from -1.75 to 1.75
- down_weight: bfloat16 [3072, 768], replicated, may hold values from -0.109375 to 0.109375
- down_bias: float32 [768], replicated, may hold values from -1.75 to 1.75
- second_gain: float32 [768], replicated, may hold values from 0.5 to 1.5
- second_shift: float32 [768], replicated, may hold values from -1.75 to 1.75
- cotangent: bfloat16 [16, 2048, 768], P('rows', 'seq'), may hold values from -18 to 18
Outputs:
- output: bfloat16 [16, 2048, 768], P('rows', 'seq')
- input_grad: float32 [16, 2048, 768], P('rows', 'seq')
- queryweight_grad: float32 [768, 768], replicated
- querybias_grad: float32 [768], replicated
- keyweight_grad: float32 [768, 768], replicated
- valueweight_grad: float32 [768, 768], replicated
- valuebias_grad: float32 [768], replicated
- outweight_grad: float32 [768, 768], replicated
- outbias_grad: float32 [768], replicated
- firstgain_grad: float32 [768], replicated
- firstshift_grad: float32 [768], replicated
- upweight_grad: float32 [768, 3072], replicated
- upbias_grad: float32 [3072], replicated
- downweight_grad: float32 [3072, 768], replicated
- downbias_grad: float32 [768], replicated
- secondgain_grad: float32 [768], replicated
- secondshift_grad: float32 [768], replicated
Inputs may be any that keep to these rules, and one draw needn't show every extreme that they name: `segments`: within each row the numbers start at 0 and never fall; in each row one segment covers a position among the first 512 and one among the last 512; some row reaches the most, 1022.
All inputs are finite; a program needn't handle non-finite values.
Results may differ from a plain program's by a relative error of at most 0.013.
Values may be sent and summed in bfloat16 or wider, within the bound.
No kernel may reach another device: no remote copies, remote signals or barrier semaphores. Data moves between devices by JAX's collectives and lax.ppermute only.
A program may use at most 512 MiB of HBM per device.

v0:
```python
from functools import partial

import jax
import jax.numpy as jnp
from jax import lax
from jax.sharding import PartitionSpec as P

HEADS = 12
HEAD = 64


EPSILON = 1e-06


def normalize(values, gain_vec, shift_vec):
    centered = values - jnp.mean(values, axis=-1, keepdims=True)
    variance = jnp.mean(centered * centered, axis=-1, keepdims=True)
    return centered * lax.rsqrt(variance + EPSILON) * gain_vec + shift_vec


def contract_rows(left, right):
    return lax.dot_general(
        left, right, (((0,), (0,)), ((), ())), preferred_element_type=jnp.float32
    )


def against_weight(left, weight):
    return lax.dot_general(
        left, weight, (((1,), (1,)), ((), ())), preferred_element_type=jnp.float32
    )


def column_sums(values):
    return jnp.sum(values.astype(jnp.float32), axis=0)


def pack_grads(grads):
    return jnp.concatenate([item.reshape(-1) for item in grads], axis=0)


def unpack_grads(packed, grads):
    pieces = []
    start = 0
    for item in grads:
        count = item.size
        pieces.append(packed[start : start + count].reshape(item.shape))
        start = start + count
    return pieces


def on_device(
    tokens,
    segments,
    query_weight,
    query_bias,
    key_weight,
    value_weight,
    value_bias,
    out_weight,
    out_bias,
    first_gain,
    first_shift,
    up_weight,
    up_bias,
    down_weight,
    down_bias,
    second_gain,
    second_shift,
    cotangent,
):
    row_count, pos_count, width = tokens.shape
    total = row_count * pos_count
    scale = HEAD ** (-0.5)
    flat = tokens.reshape(total, width)
    queries = (jnp.dot(flat, query_weight, preferred_element_type=jnp.float32) + query_bias).astype(
        jnp.bfloat16
    )
    keys_local = (
        jnp.dot(flat, key_weight, preferred_element_type=jnp.float32)
        .astype(jnp.bfloat16)
        .reshape(row_count, pos_count, width)
    )
    values_local = (
        (jnp.dot(flat, value_weight, preferred_element_type=jnp.float32) + value_bias)
        .astype(jnp.bfloat16)
        .reshape(row_count, pos_count, width)
    )
    keys_full, values_full = (
        lax.all_gather(keys_local, "seq", axis=1, tiled=True),
        lax.all_gather(values_local, "seq", axis=1, tiled=True),
    )
    seq_length = keys_full.shape[1]
    offset = lax.axis_index("seq") * pos_count
    local_segs = lax.dynamic_slice_in_dim(segments, offset, pos_count, 1)
    allowed = local_segs[:, None, :, None] == segments[:, None, None, :]
    query_heads = queries.reshape(row_count, pos_count, HEADS, HEAD)
    key_heads = keys_full.reshape(row_count, seq_length, HEADS, HEAD)
    value_heads = values_full.reshape(row_count, seq_length, HEADS, HEAD)
    scores = (
        jnp.einsum("rqhe,rkhe->rhqk", query_heads, key_heads, preferred_element_type=jnp.float32)
        * scale
    )
    scores = jnp.where(allowed, scores, -1e30)
    highest = jnp.max(scores, axis=-1, keepdims=True)
    raised = jnp.exp(scores - highest)
    totals = jnp.sum(raised, axis=-1, keepdims=True)
    logsum = highest + jnp.log(totals)
    attention_low = (raised / totals).astype(jnp.bfloat16)
    context = jnp.einsum(
        "rhqk,rkhe->rqhe", attention_low, value_heads, preferred_element_type=jnp.float32
    )
    context = context.astype(jnp.bfloat16).reshape(total, width)
    branch = jnp.dot(context, out_weight, preferred_element_type=jnp.float32) + out_bias
    hidden, first_pull = jax.vjp(
        normalize, flat.astype(jnp.float32) + branch, first_gain, first_shift
    )
    hidden_low = hidden.astype(jnp.bfloat16)
    pre_act = jnp.dot(hidden_low, up_weight, preferred_element_type=jnp.float32) + up_bias
    activated, gelu_pull = jax.vjp(partial(jax.nn.gelu, approximate=False), pre_act)
    activated_low = activated.astype(jnp.bfloat16)
    feed = jnp.dot(activated_low, down_weight, preferred_element_type=jnp.float32) + down_bias
    result, second_pull = jax.vjp(normalize, hidden + feed, second_gain, second_shift)
    output = result.astype(jnp.bfloat16).reshape(row_count, pos_count, width)
    incoming = cotangent.astype(jnp.float32).reshape(total, width)
    residual_two_grad, secondgain_grad, secondshift_grad = second_pull(incoming)
    feed_grad = residual_two_grad.astype(jnp.bfloat16)
    downweight_grad = contract_rows(activated_low, feed_grad)
    downbias_grad = column_sums(feed_grad)
    (pre_grad,) = gelu_pull(against_weight(feed_grad, down_weight))
    pre_low = pre_grad.astype(jnp.bfloat16)
    upweight_grad = contract_rows(hidden_low, pre_low)
    upbias_grad = column_sums(pre_low)
    hidden_grad = residual_two_grad + against_weight(pre_low, up_weight)
    residual_one_grad, firstgain_grad, firstshift_grad = first_pull(hidden_grad)
    branch_low = residual_one_grad.astype(jnp.bfloat16)
    outweight_grad = contract_rows(context, branch_low)
    outbias_grad = column_sums(branch_low)
    context_grad = (
        against_weight(branch_low, out_weight)
        .astype(jnp.bfloat16)
        .reshape(row_count, pos_count, HEADS, HEAD)
    )
    rescored = (
        jnp.einsum("rqhe,rkhe->rhqk", query_heads, key_heads, preferred_element_type=jnp.float32)
        * scale
    )
    rescored = jnp.where(allowed, rescored, -1e30)
    attention = jnp.exp(rescored - logsum)
    attention_again = attention.astype(jnp.bfloat16)
    prob_grad = jnp.einsum(
        "rqhe,rkhe->rhqk", context_grad, value_heads, preferred_element_type=jnp.float32
    )
    value_part = jnp.einsum(
        "rhqk,rqhe->rkhe", attention_again, context_grad, preferred_element_type=jnp.float32
    )
    inner = jnp.sum(prob_grad * attention, axis=-1, keepdims=True)
    score_grad = (attention * (prob_grad - inner)).astype(jnp.bfloat16)
    query_part = (
        jnp.einsum("rhqk,rkhe->rqhe", score_grad, key_heads, preferred_element_type=jnp.float32)
        * scale
    )
    key_part = (
        jnp.einsum("rhqk,rqhe->rkhe", score_grad, query_heads, preferred_element_type=jnp.float32)
        * scale
    )
    key_sum, value_sum = (
        lax.psum_scatter(
            key_part.reshape(row_count, seq_length, width), "seq", scatter_dimension=1, tiled=True
        ),
        lax.psum_scatter(
            value_part.reshape(row_count, seq_length, width), "seq", scatter_dimension=1, tiled=True
        ),
    )
    query_low = query_part.reshape(total, width).astype(jnp.bfloat16)
    key_low = key_sum.reshape(total, width).astype(jnp.bfloat16)
    value_low = value_sum.reshape(total, width).astype(jnp.bfloat16)
    queryweight_grad = contract_rows(flat, query_low)
    querybias_grad = column_sums(query_low)
    keyweight_grad = contract_rows(flat, key_low)
    valueweight_grad = contract_rows(flat, value_low)
    valuebias_grad = column_sums(value_low)
    input_grad = (
        residual_one_grad
        + against_weight(query_low, query_weight)
        + against_weight(key_low, key_weight)
        + against_weight(value_low, value_weight)
    )
    input_grad = input_grad.reshape(row_count, pos_count, width)
    grads = (
        queryweight_grad,
        querybias_grad,
        keyweight_grad,
        valueweight_grad,
        valuebias_grad,
        outweight_grad,
        outbias_grad,
        firstgain_grad,
        firstshift_grad,
        upweight_grad,
        upbias_grad,
        downweight_grad,
        downbias_grad,
        secondgain_grad,
        secondshift_grad,
    )
    packed = pack_grads(grads)
    shares = lax.psum_scatter(packed, ("rows", "seq"), scatter_dimension=0, tiled=True)
    summed_flat = lax.all_gather(shares, ("rows", "seq"), axis=0, tiled=True)
    summed = unpack_grads(summed_flat, grads)
    return (
        output,
        input_grad,
        summed[0],
        summed[1],
        summed[2],
        summed[3],
        summed[4],
        summed[5],
        summed[6],
        summed[7],
        summed[8],
        summed[9],
        summed[10],
        summed[11],
        summed[12],
        summed[13],
        summed[14],
    )


def solution(mesh):
    return jax.shard_map(
        on_device,
        mesh=mesh,
        in_specs=(
            P("rows", "seq", None),
            P("rows", None),
            P(),
            P(),
            P(),
            P(),
            P(),
            P(),
            P(),
            P(),
            P(),
            P(),
            P(),
            P(),
            P(),
            P(),
            P(),
            P("rows", "seq", None),
        ),
        out_specs=(
            P("rows", "seq", None),
            P("rows", "seq", None),
            P(),
            P(),
            P(),
            P(),
            P(),
            P(),
            P(),
            P(),
            P(),
            P(),
            P(),
            P(),
            P(),
            P(),
            P(),
        ),
        check_vma=False,
    )
```

profile of v0, /device:TPU:0, one launch (start us, length us, event | category | flops | bytes accessed | tf_op | source)
XLA Modules:
  0.0 1865.2 jit_solution(1760269803548899115)
XLA Ops:
  7.3 4.4 convolution_convert_fusion.1
  11.8 3.9 add_convert_fusion.3
  17.4 5.0 add_convert_fusion.2
  25.2 3.9 reshape.240
  29.1 31.9 %all-gather.5.cloned.1.call-done = bf16[2,2048,768]{2,1,0:T(8,128)(2,1)} async-done(((bf16[2,512,768]{2,1,0:T(8,128)(2,1)}), bf16[2,2048,768]{2,1,0:T(8,128)(2,1)}) %all-gather.5.cloned.1.call-update) | async-done | bytes 6291472 | tf_op jit(solution)/shard_map/all_gather | solution.py:89
  61.0 8.6 copy.60
  69.6 38.5 %fusion.6 = (f32[2,12,512]{2,1,0:T(8,128)S(1)}, f32[2,12,512,2048]{3,2,1,0:T(8,128)}) fusion(pred[2,512,2048]{2,1,0:T(8,128)(4,1)S(1)} %broadcast_compare_fusion, bf16[2,2048,12,64]{1,3,2,0:T(8,128)(2,1)} %bitcast.100, bf16[2,512,12,64]{1,0,3,2:T(2,128)(2,1)} %reshape.240), kind=kOutput, calls=%fused_computation.11 | convolution fusion | flops 3296710656 | bytes 110673920 | tf_op jit(solution)/shard_map/rqhe,rkhe->rhqk/dot_general | solution.py:100
  108.1 31.4 %fusion = f32[2,12,512]{2,1,0:T(8,128)S(1)} fusion(f32[2,12,512]{2,1,0:T(8,128)S(1)} %get-tuple-element.49, f32[2,12,512,2048]{3,2,1,0:T(8,128)} %get-tuple-element.50, pred[2,512,2048]{2,1,0:T(8,128)(4,1)S(1)} %broadcast_compare_fusion), kind=kLoop, calls=%fused_computation.6 | loop fusion | flops 100651008 | bytes 102858752 | tf_op jit(solution)/shard_map/reduce_sum | solution.py:106
  140.2 8.6 copy.58
  148.8 38.4 %fusion.19 = bf16[2,512,12,64]{1,3,2,0:T(8,128)(2,1)S(1)} fusion(bf16[2,2048,12,64]{1,3,2,0:T(8,128)(2,1)} %bitcast.104, f32[2,12,512]{2,1,0:T(8,128)S(1)} %fusion, f32[2,12,512]{2,1,0:T(8,128)S(1)} %get-tuple-element.49, f32[2,12,512,2048]{3,2,1,0:T(8,128)} %get-tuple-element.50, pred[2,512,2048]{2,1,0:T(8,128)(4,1)S(1)} %broadcast_compare_fusion), kind=kOutput, calls=%fused_computation.68 | convolution fusion | flops 3347841024 | bytes 110723072 | tf_op jit(solution)/shard_map/rhqk,rkhe->rqhe/dot_general | solution.py:109
  193.7 35.4 %multiply_convert_fusion.1 = (bf16[1024,3072]{1,0:T(8,128)(2,1)S(1)}, f32[1024,3072]{1,0:T(8,128)}, f32[1024,3072]{1,0:T(8,128)}) fusion(f32[3072]{0:T(1024)S(1)} %copy-done.48, bf16[768,3072]{1,0:T(8,128)(2,1)S(1)} %bitcast.122, f32[1024,768]{1,0:T(8,128)S(1)} %get-tuple-element.52, f32[768]{0:T(1024)S(1)} %copy-done.29, f32[768]{0:T(1024)S(1)} %copy-done.27, ...), kind=kOutput, calls=%fused_computation.16 | convolution fusion | flops 5043388416 | bytes 39348224 | tf_op jit(solution)/shard_map/dot_general | solution.py:118
  229.1 5.5 fusion.43
  243.0 17.9 convert_reduce_fusion
  260.9 10.8 multiply_reduce_fusion.1
  280.9 3.8 reshape.246
  284.7 75.7 %multiply_reduce_fusion = (f32[2,12,512]{2,1,0:T(8,128)S(1)}, f32[2,12,512,2048]{3,2,1,0:T(8,128)}) fusion(f32[2,12,512]{2,1,0:T(8,128)S(1)} %copy-done.12, f32[2,12,512,2048]{3,2,1,0:T(8,128)} %get-tuple-element.50, pred[2,512,2048]{2,1,0:T(8,128)(4,1)S(1)} %copy-done.3, bf16[2,2048,12,64]{1,3,2,0:T(8,128)(2,1)} %bitcast.105, ...), kind=kOutput, calls=%fused_computation.1 | convolution fusion | flops 3347042304 | bytes 211386368 | tf_op jit(solution)/shard_map/rqhe,rkhe->rhqk/dot_general | solution.py:150
  360.5 78.0 %multiply_convert_fusion = bf16[2,12,512,2048]{3,2,1,0:T(8,128)(2,1)} fusion(f32[2,12,512,2048]{3,2,1,0:T(8,128)} %get-tuple-element.58, f32[2,12,512]{2,1,0:T(8,128)S(1)} %get-tuple-element.57, f32[2,12,512]{2,1,0:T(8,128)S(1)} %copy-done.12, f32[2,12,512,2048]{3,2,1,0:T(8,128)} %get-tuple-element.50, pred[2,512,2048]{2,1,0:T(8,128)(4,1)S(1)} %copy-done.3), kind=kLoop, calls=%fused_computation | loop fusion | flops 150994944 | bytes 253853696 | tf_op jit(solution)/shard_map/convert_element_type | solution.py:157
  438.5 23.0 %broadcast_multiply_fusion = f32[2,12,64,2048]{3,2,1,0:T(8,128)} fusion(bf16[2,12,512,2048]{3,2,1,0:T(8,128)(2,1)} %multiply_convert_fusion, bf16[2,512,12,64]{1,0,3,2:T(2,128)(2,1)} %reshape.240), kind=kOutput, calls=%fused_computation.30 | convolution fusion | flops 3224371200 | bytes 64487424 | tf_op jit(solution)/shard_map/rhqk,rqhe->rkhe/dot_general | solution.py:163
  461.6 12.6 copy.67
  474.2 47.7 %fusion.2 = f32[2,12,64,2048]{3,2,1,0:T(8,128)} fusion(f32[2,12,512]{2,1,0:T(8,128)S(1)} %copy-done.12, f32[2,12,512,2048]{3,2,1,0:T(8,128)} %get-tuple-element.50, pred[2,512,2048]{2,1,0:T(8,128)(4,1)S(1)} %copy-done.3, bf16[2,512,12,64]{1,0,3,2:T(2,128)(2,1)} %reshape.246), kind=kOutput, calls=%fused_computation.8 | convolution fusion | flops 3321888768 | bytes 116965376 | tf_op jit(solution)/shard_map/rhqk,rqhe->rkhe/dot_general | solution.py:153
  521.9 13.0 copy.69
  536.5 23.5 %convert_reduce_fusion.5 = (f32[12,64]{1,0:T(8,128)S(1)}, bf16[2,512,12,64]{1,3,2,0:T(8,128)(2,1)S(1)}) fusion(bf16[2,2048,12,64]{1,3,2,0:T(8,128)(2,1)} %bitcast.101, bf16[2,12,512,2048]{3,2,1,0:T(8,128)(2,1)} %multiply_convert_fusion), kind=kOutput, calls=%fused_computation.46 | convolution fusion | flops 3224370432 | bytes 58199040 | tf_op jit(solution)/shard_map/rhqk,rkhe->rqhe/dot_general | solution.py:159
  569.7 4.7 fusion.46
  576.8 9.1 convolution_bitcast_fusion
  585.9 7.7 copy.79
  593.7 10.6 fusion.47
  604.3 11.0 reshape.255
  615.3 3.6 constant_dynamic-update-slice_fusion.9
  629.4 3.2 reshape.251
  632.6 42.3 %reduce-scatter.5.cloned.1.call-done = f32[2,512,768]{2,1,0:T(8,128)} async-done(((f32[2,2048,768]{2,1,0:T(8,128)}), f32[2,512,768]{2,1,0:T(8,128)}) %reduce-scatter.5.cloned.1.call-update) | async-done | bytes 3145744 | tf_op jit(solution)/shard_map/reduce_scatter | solution.py:170
  684.4 3.2 reshape.252
  687.6 21.3 %dynamic-update-slice.3 = f32[7087104]{0:T(1024)} dynamic-update-slice(f32[7087104]{0:T(1024)} %constant_dynamic-update-slice_fusion.8, f32[589824]{0:T(1024)} %reshape.251, s32[]{} %constant.107) | dynamic-update-slice | bytes 4718596
  708.8 21.2 %dynamic-update-slice.4 = f32[7087104]{0:T(1024)} dynamic-update-slice(f32[7087104]{0:T(1024)} %dynamic-update-slice.3, f32[589824]{0:T(1024)} %reshape.252, s32[]{} %constant.108) | dynamic-update-slice | bytes 4718596
  731.4 20.3 %dynamic-update-slice.6 = f32[7087104]{0:T(1024)} dynamic-update-slice(f32[7087104]{0:T(1024)} %constant_dynamic-update-slice_fusion.7, f32[589824]{0:T(1024)S(1)} %reshape.253, s32[]{} %constant.110) | dynamic-update-slice | bytes 4718596
  755.6 80.4 %dynamic-update-slice.10 = f32[7087104]{0:T(1024)} dynamic-update-slice(f32[7087104]{0:T(1024)} %constant_dynamic-update-slice_fusion.4, f32[2359296]{0:T(1024)} %bitcast.103, s32[]{} %constant.114) | dynamic-update-slice | bytes 18874372
  837.3 80.4 %dynamic-update-slice.12 = f32[7087104]{0:T(1024)} dynamic-update-slice(f32[7087104]{0:T(1024)} %constant_dynamic-update-slice_fusion.3, f32[2359296]{0:T(1024)} %reshape.255, s32[]{} %constant.116) | dynamic-update-slice | bytes 18874372
  921.7 433.5 %all-reduce.7.cloned.1.call-done = f32[7087104]{0:T(1024)} async-done(((f32[7087104]{0:T(1024)}), f32[7087104]{0:T(1024)}) %all-reduce.7.cloned.1.call-update) | async-done | bytes 28348432
  1355.2 9.6 broadcast.122
  1364.8 3.0 dynamic-slice_dynamic-update-slice_fusion
  1375.3 3.1 add_add_fusion.2
  1378.5 421.8 %all-reduce.5.cloned.1.call-done = f32[7087104]{0:T(1024)} async-done(((f32[7087104]{0:T(1024)}), f32[7087104]{0:T(1024)}) %all-reduce.5.cloned.1.call-update) | async-done | bytes 28348432
  1800.3 6.9 fusion.41
  1807.2 3.4 slice.96
  1810.6 3.4 slice.99
  1813.9 3.4 slice.101
  1818.9 14.2 fusion.40
  1833.1 10.9 reshape.256
  1844.0 11.4 slice.111
  (184 shorter events, 85.0 us)
Async XLA Ops:
  7.2 182.1 %copy-start = (bf16[768,768]{1,0:T(8,128)(2,1)S(1)}, bf16[768,768]{1,0:T(8,128)(2,1)}, u32[]{:S(2)}) copy-start(bf16[768,768]{1,0:T(8,128)(2,1)} %param.25) | copy-start | bytes 3538948
  7.2 53.8 %all-gather.5.cloned.1.call-start = ((), (), s32[]{:S(2)}) async-start(), calls=%async_computation.3 | async-start | bytes 7864320 | tf_op jit(solution)/shard_map/all_gather | solution.py:89
  7.3 4.5 copy-start.21
  7.3 4.5 copy-start.49
  11.7 4.3 copy-start.33
  11.7 128.4 %all-gather.3.cloned.1.call-start = ((), (), s32[]{:S(2)}) async-start(), calls=%async_computation.2 | async-start | bytes 7864320 | tf_op jit(solution)/shard_map/all_gather | solution.py:90
  15.8 604.4 %reduce-scatter.3.cloned.1.call-start = ((), (), s32[]{:S(2)}) async-start(), calls=%async_computation.4 | async-start | bytes 15728640 | tf_op jit(solution)/shard_map/reduce_scatter | solution.py:167
  17.4 131.4 %copy-start.2 = (pred[2,512,2048]{2,1,0:T(8,128)(4,1)}, pred[2,512,2048]{2,1,0:T(8,128)(4,1)S(1)}, u32[]{:S(2)}) copy-start(pred[2,512,2048]{2,1,0:T(8,128)(4,1)S(1)} %broadcast_compare_fusion) | copy-start | bytes 6291460
  187.2 2.1 copy-start.42
  187.2 2.1 copy-start.51
  189.2 2.9 slice-start.2
  189.3 3.4 slice-start.3
  189.3 39.8 %slice-start = ((s8[4718592]{0:T(1024)(128)(4,1)}), s8[4194304]{0:T(1024)(128)(4,1)S(1)}, s32[]{:S(2)}) async-start(s8[4718592]{0:T(1024)(128)(4,1)} %bitcast.119), calls=%async_computation.8 | async-start | bytes 8388608
  191.0 80.7 %copy-start.4 = (f32[1024,768]{1,0:T(8,128)}, f32[1024,768]{1,0:T(8,128)S(1)}, u32[]{:S(2)}) copy-start(f32[1024,768]{1,0:T(8,128)S(1)} %get-tuple-element.52) | copy-start | bytes 9437188
  191.0 2.6 copy-start.27
  191.0 2.6 copy-start.29
  191.0 2.6 copy-start.48
  191.1 80.6 %copy-start.23 = (f32[1024]{0:T(1024)}, f32[1024]{0:T(1024)S(1)}, u32[]{:S(2)}) copy-start(f32[1024]{0:T(1024)S(1)} %broadcast_multiply_fusion.2) | copy-start | bytes 12292
  193.7 78.0 %copy-start.25 = (f32[1024]{0:T(1024)}, f32[1024]{0:T(1024)S(1)}, u32[]{:S(2)}) copy-start(f32[1024]{0:T(1024)S(1)} %fusion.27) | copy-start | bytes 12292
  193.7 35.4 %slice-start.1 = ((s8[4718592]{0:T(1024)(128)(4,1)}), s8[524288]{0:T(1024)(128)(4,1)S(1)}, s32[]{:S(2)}) async-start(s8[4718592]{0:T(1024)(128)(4,1)} %bitcast.119), calls=%async_computation.9 | async-start | bytes 1048576
  193.7 35.4 %copy-start.52 = (f32[768]{0:T(1024)S(1)}, f32[768]{0:T(1024)}, u32[]{:S(2)}) copy-start(f32[768]{0:T(1024)} %param.32) | copy-start | bytes 9220
  229.1 5.5 copy-start.53
  235.2 2.6 copy-start.39
  243.0 17.9 copy-start.18
  278.2 6.6 copy-start.3
  278.2 6.6 copy-start.12
  474.2 200.8 %reduce-scatter.5.cloned.1.call-start = ((), (), s32[]{:S(2)}) async-start(), calls=%async_computation.5 | async-start | bytes 15728640 | tf_op jit(solution)/shard_map/reduce_scatter | solution.py:170
  534.9 820.3 %all-reduce.7.cloned.1.call-start = ((), (), s32[]{:S(2)}) async-start(), calls=%async_computation.7 | async-start | bytes 56696832
  560.0 3.2 copy-start.43
  574.4 2.4 copy-start.24
  574.4 2.4 copy-start.26
  574.4 2.4 copy-start.28
  574.4 2.4 copy-start.30
  585.9 7.8 copy-start.19
  620.1 3.3 copy-start.44
  674.9 3.5 copy-start.45
  730.1 21.6 %copy-start.35 = (f32[768]{0:T(1024)S(1)}, f32[768]{0:T(1024)}, u32[]{:S(2)}) copy-start(f32[768]{0:T(1024)} %get-tuple-element.24) | copy-start | bytes 9220
  730.1 22.9 %copy-start.41 = (f32[768]{0:T(1024)S(1)}, f32[768]{0:T(1024)}, u32[]{:S(2)}) copy-start(f32[768]{0:T(1024)} %get-tuple-element.17) | copy-start | bytes 9220
  730.1 24.2 %copy-start.40 = (f32[768]{0:T(1024)S(1)}, f32[768]{0:T(1024)}, u32[]{:S(2)}) copy-start(f32[768]{0:T(1024)} %get-tuple-element.21) | copy-start | bytes 9220
  755.6 80.4 %copy-start.38 = (f32[3072]{0:T(1024)S(1)}, f32[3072]{0:T(1024)}, u32[]{:S(2)}) copy-start(f32[3072]{0:T(1024)} %get-tuple-element.61) | copy-start | bytes 36868
  837.3 80.4 %copy-start.34 = (f32[768]{0:T(1024)S(1)}, f32[768]{0:T(1024)}, u32[]{:S(2)}) copy-start(f32[768]{0:T(1024)} %get-tuple-element.22) | copy-start | bytes 9220
  837.3 81.7 %copy-start.37 = (f32[768]{0:T(1024)S(1)}, f32[768]{0:T(1024)}, u32[]{:S(2)}) copy-start(f32[768]{0:T(1024)} %get-tuple-element.19) | copy-start | bytes 9220
  921.6 878.7 %all-reduce.5.cloned.1.call-start = ((), (), s32[]{:S(2)}) async-start(), calls=%async_computation.6 | async-start | bytes 56696832
  1371.3 2.7 copy-start.6
  1371.3 3.6 copy-start.11
  1371.3 4.0 copy-start.22
  1371.3 4.0 copy-start.32
  1844.0 14.1 copy-start.1
  (16 other events, 23.6 us)
Sparse Core Ops, SparseCore 0:
  11.8 49.0 all-gather.4
  63.1 46.3 all-gather.2
  474.3 99.0 reduce-scatter.2
  575.8 99.0 reduce-scatter.4
  921.8 433.3 all-reduce.6
  1368.0 432.2 all-reduce.4
where the time goes:
time: 1890 us; the launch traced here: 1870 us
  waiting for transfers between devices  930 us (49%)
  local copies, waits for them, and re-layouts  422 us (22%)
  matrix products  373 us (20%)
  other arithmetic  125 us (7%)
    unnamed x8, waiting for transfers between devices  855 us
    unnamed x135, local copies, waits for them, and re-layouts  274 us
    convert_element_type x1, other arithmetic, on_device(): score_grad = (attention * (prob_grad - inner)).astype(jnp.bfloat16)  78 us
    dot_general x1, matrix products, on_device(): jnp.einsum('rqhe,rkhe->rhqk', context_grad, value_heads, preferred_elemen...  75.7 us
    dot_general x1, matrix products, on_device(): jnp.einsum('rhqk,rqhe->rkhe', attention_again, context_grad, preferred_el...  47.7 us
    slice x9, local copies, waits for them, and re-layouts, unpack_grads(): pieces.append(packed[start:start + count].reshape(item.shape))  46.9 us
    reduce_scatter x1, waiting for transfers between devices, on_device(): lax.psum_scatter(value_part.reshape(row_count, seq_length, width), 'seq',...  42.3 us
    dot_general x1, matrix products, on_device(): jnp.einsum('rqhe,rkhe->rhqk', query_heads, key_heads, preferred_element_t...  38.5 us
  transfers between devices with their start and end apart: 6, of which 4 were waited for; matrix products, arithmetic and copies ran while one was open for 14% of the time, Pallas kernels for 0%

commit v1 on v0

v1 whole, which is shorter than its diff:
```python
import functools
import math

import jax
import jax.numpy as jnp
from jax import lax
from jax.experimental import pallas as pl
from jax.experimental.pallas import tpu as pltpu
from jax.sharding import PartitionSpec as P

HEADS = 12
HEAD = 64
PAIR = 2 * HEAD
EPSILON = 1e-06
BLOCKED = -(2.0**100)
VMEM_LIMIT = 60 * 2**20
bf16 = jnp.bfloat16
f32 = jnp.float32


def dot(left, right, over_left, over_right):
    return lax.dot_general(
        left, right, (((over_left,), (over_right,)), ((), ())), preferred_element_type=f32
    )


def attention_forward_kernel(
    block, piece, q_ref, k_ref, v_ref, qmark_ref, kmark_ref, segq_ref, segk_ref,
    ctx_ref, prob_ref, inv_ref, keys, vals, scores,
):
    step = pl.program_id(1)
    lane = lax.broadcasted_iota(jnp.int32, (1, PAIR), 1)
    low = lane < HEAD
    factor = HEAD**-0.5 * math.log2(math.e)

    @pl.when(step == 0)
    def _():
        k, v, mark = k_ref[...], v_ref[...], kmark_ref[...]
        one = jnp.ones_like(v)
        keys[0] = jnp.where(low, k, mark)
        keys[1] = jnp.where(low, mark, k)
        vals[0] = jnp.where(low, v, one)
        vals[1] = jnp.where(low, one, v)

    q, mark = q_ref[...], qmark_ref[...]
    zero = jnp.zeros_like(q)
    own = (step * block) // piece
    start = pl.multiple_of(own * piece, piece)
    same = segq_ref[...] == segk_ref[0, pl.ds(own, 1), :]
    for h in range(2):
        keep = low if h == 0 else jnp.logical_not(low)
        scores[h] = dot(jnp.where(keep, q, mark), keys[h], 1, 1)
        near = dot(jnp.where(keep, q, zero), keys[h, pl.ds(start, piece), :], 1, 1)
        scores[h, :, pl.ds(start, piece)] = jnp.where(same, near, BLOCKED)
    sums = []
    for h in range(2):
        highest = jnp.max(scores[h], axis=1, keepdims=True) * factor
        prob = jnp.exp2(scores[h] * factor - highest).astype(bf16)
        prob_ref[h] = prob
        sums.append(dot(prob, vals[h], 1, 0))
    total = pltpu.roll(jnp.where(low, sums[1], sums[0]), HEAD, 1)
    inverse = 1.0 / total
    ctx_ref[...] = (jnp.where(low, sums[0], sums[1]) * inverse).astype(bf16)
    inv_ref[...] = inverse


def attention_forward(qkv, qmark, kmark, segq, segk, block=512):
    length, width = qkv.shape[0], qkv.shape[1] // 3
    pairs, piece = width // PAIR, segk.shape[-1]
    row = pl.BlockSpec((block, PAIR), lambda p, b: (b, p))
    return pl.pallas_call(
        functools.partial(attention_forward_kernel, block, piece),
        grid=(pairs, length // block),
        in_specs=[
            row,
            pl.BlockSpec((length, PAIR), lambda p, b: (0, pairs + p)),
            pl.BlockSpec((length, PAIR), lambda p, b: (0, 2 * pairs + p)),
            pl.BlockSpec((block, PAIR), lambda p, b: (b, 0)),
            pl.BlockSpec((length, PAIR), lambda p, b: (0, 0)),
            pl.BlockSpec((block, 1), lambda p, b: (b, 0)),
            pl.BlockSpec((1, length // piece, piece), lambda p, b: (0, 0, 0)),
        ],
        out_specs=[row, pl.BlockSpec((2, block, length), lambda p, b: (p, b, 0)), row],
        out_shape=[
            jax.ShapeDtypeStruct((length, width), bf16),
            jax.ShapeDtypeStruct((width // HEAD, length, length), bf16),
            jax.ShapeDtypeStruct((length, width), f32),
        ],
        scratch_shapes=[
            pltpu.VMEM((2, length, PAIR), bf16),
            pltpu.VMEM((2, length, PAIR), bf16),
            pltpu.VMEM((2, block, length), f32),
        ],
        compiler_params=pltpu.CompilerParams(vmem_limit_bytes=VMEM_LIMIT),
        cost_estimate=pl.CostEstimate(
            flops=16 * length * length * width,
            bytes_accessed=2 * length * length * (width // HEAD),
            transcendentals=length * length * (width // HEAD),
        ),
        name="attention_forward",
    )(qkv, qkv, qkv, qmark, kmark, segq, segk)


def attention_backward_kernel(
    chunk, do_ref, ctx_ref, inv_ref, q_ref, k_ref, v_ref, prob_ref,
    dq_ref, dk_ref, dv_ref, vals, dkeys, dvals,
):
    step, steps = pl.program_id(1), pl.num_programs(1)
    length = k_ref.shape[0]
    lane = lax.broadcasted_iota(jnp.int32, (1, PAIR), 1)
    low = lane < HEAD
    slot = jnp.bitwise_and(lane, HEAD - 1)
    scale = HEAD**-0.5

    @pl.when(step == 0)
    def _():
        v = v_ref[...]
        mark = jnp.broadcast_to((slot < 3).astype(f32), v.shape).astype(bf16)
        vals[0] = jnp.where(low, v, mark)
        vals[1] = jnp.where(low, mark, v)
        dkeys[...] = jnp.zeros_like(dkeys)
        dvals[...] = jnp.zeros_like(dvals)

    grad = (do_ref[...].astype(f32) * inv_ref[...]).astype(bf16)
    product = grad.astype(f32) * ctx_ref[...].astype(f32)
    grad_t, q_t = grad.T, q_ref[...].T
    dqs = []
    for h in range(2):
        keep = low if h == 0 else jnp.logical_not(low)
        inner = jnp.sum(jnp.where(keep, product, 0.0), axis=1, keepdims=True)
        top = inner.astype(bf16).astype(f32)
        mid = (inner - top).astype(bf16).astype(f32)
        rest = inner - top - mid
        mark = jnp.where(slot == 0, -top, jnp.where(slot == 1, -mid, jnp.where(slot == 2, -rest, 0.0)))
        left = jnp.where(keep, grad, mark.astype(bf16))
        part = slice(h * HEAD, (h + 1) * HEAD)
        dq = None
        for j in range(length // chunk):
            cols = slice(j * chunk, (j + 1) * chunk)
            prob = prob_ref[h, :, cols]
            ds = prob * dot(left, vals[h, cols, :], 1, 1).astype(bf16)
            dvals[part, cols] += dot(grad_t[part], prob, 1, 0)
            dkeys[part, cols] += dot(q_t[part], ds, 1, 0)
            term = dot(ds, k_ref[cols, :], 1, 0)
            dq = term if dq is None else dq + term
        dqs.append(dq)
    dq_ref[...] = (jnp.where(low, dqs[0], dqs[1]) * scale).astype(bf16)

    @pl.when(step == steps - 1)
    def _():
        dk_ref[...] = (dkeys[...] * scale).T.astype(bf16)
        dv_ref[...] = dvals[...].T.astype(bf16)


def attention_backward(pair, grad, ctx, inv, qkv, prob, block=512, chunk=512):
    length, width = ctx.shape
    pairs = width // PAIR
    row = pl.BlockSpec((block, PAIR), lambda p, b: (b, pair))
    full = pl.BlockSpec((length, PAIR), lambda p, b: (0, 0))
    shape = jax.ShapeDtypeStruct((length, PAIR), bf16)
    return pl.pallas_call(
        functools.partial(attention_backward_kernel, chunk),
        grid=(1, length // block),
        in_specs=[
            row,
            row,
            row,
            row,
            pl.BlockSpec((length, PAIR), lambda p, b: (0, pairs + pair)),
            pl.BlockSpec((length, PAIR), lambda p, b: (0, 2 * pairs + pair)),
            pl.BlockSpec((2, block, length), lambda p, b: (pair, b, 0)),
        ],
        out_specs=[pl.BlockSpec((block, PAIR), lambda p, b: (b, 0)), full, full],
        out_shape=[shape, shape, shape],
        scratch_shapes=[
            pltpu.VMEM((2, length, PAIR), bf16),
            pltpu.VMEM((PAIR, length), f32),
            pltpu.VMEM((PAIR, length), f32),
        ],
        compiler_params=pltpu.CompilerParams(vmem_limit_bytes=VMEM_LIMIT),
        cost_estimate=pl.CostEstimate(
            flops=32 * length * length * PAIR,
            bytes_accessed=4 * length * length,
            transcendentals=0,
        ),
        name="attention_backward",
    )(grad, ctx, inv, qkv, qkv, qkv, prob)


def norm_stats(values):
    centered = values - jnp.mean(values, axis=-1, keepdims=True)
    inverse = lax.rsqrt(jnp.mean(centered * centered, axis=-1, keepdims=True) + EPSILON)
    return centered * inverse, inverse


def norm_backward(grad, gain, normed, inverse):
    t = grad * gain
    return (
        t - jnp.mean(t, axis=-1, keepdims=True) - normed * jnp.mean(t * normed, axis=-1, keepdims=True)
    ) * inverse


def row_sum(values):
    return jnp.sum(values, axis=0, keepdims=True)


def feed_forward_kernel(
    chunk, ctx_a_ref, ctx_b_ref, tok_ref, cot_ref, wo_ref, wu_ref, wd_ref, bo_ref, g1_ref, s1_ref,
    bu_ref, bd_ref, g2_ref, s2_ref, out_ref, act_ref, slope_ref, r2_ref, feed_ref, n1_ref, hid_ref, inv_ref,
    sums_ref,
):
    @pl.when(pl.program_id(0) == 0)
    def _():
        sums_ref[...] = jnp.zeros_like(sums_ref)

    split = ctx_a_ref.shape[1]
    branch = dot(ctx_a_ref[...], wo_ref[:split], 1, 0)
    if split < wo_ref.shape[0]:
        branch += dot(ctx_b_ref[...], wo_ref[split:], 1, 0)
    n1, inv1 = norm_stats(tok_ref[...].astype(f32) + branch + bo_ref[...])
    hidden = n1 * g1_ref[...] + s1_ref[...]
    low = hidden.astype(bf16)
    n1_ref[...] = n1
    inv_ref[...] = inv1
    hid_ref[...] = low
    total = hidden + bd_ref[...]
    for j in range(wu_ref.shape[1] // chunk):
        cols = slice(j * chunk, (j + 1) * chunk)
        pre = dot(low, wu_ref[:, cols], 1, 0) + bu_ref[:, cols]
        phi = jnp.exp(pre * pre * -0.5) * (1.0 / math.sqrt(2.0 * math.pi))
        cdf = 0.5 + 0.5 * lax.erf(pre * math.sqrt(0.5))
        act = (pre * cdf).astype(bf16)
        act_ref[:, cols] = act
        slope_ref[:, cols] = (cdf + pre * phi).astype(bf16)
        total += dot(act, wd_ref[cols, :], 1, 0)
    n2, inv2 = norm_stats(total)
    out_ref[...] = (n2 * g2_ref[...] + s2_ref[...]).astype(bf16)
    grad = cot_ref[...].astype(f32)
    r2 = norm_backward(grad, g2_ref[...], n2, inv2)
    feed = r2.astype(bf16)
    r2_ref[...] = r2
    feed_ref[...] = feed
    sums_ref[0:1] += row_sum(grad * n2)
    sums_ref[1:2] += row_sum(grad)
    sums_ref[2:3] += row_sum(feed.astype(f32))


def feed_backward_kernel(
    chunk, r2_ref, feed_ref, slope_ref, n1_ref, inv_ref, wo_ref, wu_ref, wd_ref, g1_ref,
    pre_ref, r1_ref, branch_ref, dctx_ref, sums_ref, upsum_ref,
):
    @pl.when(pl.program_id(0) == 0)
    def _():
        sums_ref[...] = jnp.zeros_like(sums_ref)
        upsum_ref[...] = jnp.zeros_like(upsum_ref)

    feed = feed_ref[...]
    grad = r2_ref[...]
    for j in range(wu_ref.shape[1] // chunk):
        cols = slice(j * chunk, (j + 1) * chunk)
        pre = (dot(feed, wd_ref[cols, :], 1, 1) * slope_ref[:, cols].astype(f32)).astype(bf16)
        pre_ref[:, cols] = pre
        upsum_ref[0:1, cols] += row_sum(pre.astype(f32))
        grad += dot(pre, wu_ref[:, cols], 1, 1)
    n1 = n1_ref[...]
    r1 = norm_backward(grad, g1_ref[...], n1, inv_ref[...])
    branch = r1.astype(bf16)
    r1_ref[...] = r1
    branch_ref[...] = branch
    dctx_ref[...] = dot(branch, wo_ref[...], 1, 1).astype(bf16)
    sums_ref[0:1] += row_sum(grad * n1)
    sums_ref[1:2] += row_sum(grad)
    sums_ref[2:3] += row_sum(branch.astype(f32))


def whole(shape):
    return pl.BlockSpec(shape, lambda i: (0,) * len(shape), pipeline_mode=pl.Buffered(1))


def feed_forward(ctx_a, ctx_b, tok, cot, wo, wu, wd, bo, g1, s1, bu, bd, g2, s2, block=256):
    count, width = tok.shape
    hidden = wu.shape[1]
    rows = lambda n: pl.BlockSpec((block, n), lambda i: (i, 0))
    return pl.pallas_call(
        functools.partial(feed_forward_kernel, 768),
        grid=(count // block,),
        in_specs=[rows(ctx_a.shape[1]), rows(ctx_b.shape[1]), rows(width), rows(width)]
        + [whole(x.shape) for x in (wo, wu, wd, bo, g1, s1, bu, bd, g2, s2)],
        out_specs=[rows(width), rows(hidden), rows(hidden), rows(width), rows(width), rows(width), rows(width), rows(1),
                   pl.BlockSpec((8, width), lambda i: (0, 0))],
        out_shape=[
            jax.ShapeDtypeStruct((count, width), bf16),
            jax.ShapeDtypeStruct((count, hidden), bf16),
            jax.ShapeDtypeStruct((count, hidden), bf16),
            jax.ShapeDtypeStruct((count, width), f32),
            jax.ShapeDtypeStruct((count, width), bf16),
            jax.ShapeDtypeStruct((count, width), f32),
            jax.ShapeDtypeStruct((count, width), bf16),
            jax.ShapeDtypeStruct((count, 1), f32),
            jax.ShapeDtypeStruct((8, width), f32),
        ],
        compiler_params=pltpu.CompilerParams(vmem_limit_bytes=VMEM_LIMIT),
        cost_estimate=pl.CostEstimate(
            flops=2 * count * width * (width + 2 * hidden), bytes_accessed=40 * 2**20, transcendentals=2 * count * hidden
        ),
        name="feed_forward",
    )(ctx_a, ctx_b, tok, cot, wo, wu, wd, bo, g1, s1, bu, bd, g2, s2)


def feed_backward(r2, feed, slope, n1, inv, wo, wu, wd, g1, block=256):
    count, width = r2.shape
    hidden = wu.shape[1]
    rows = lambda n: pl.BlockSpec((block, n), lambda i: (i, 0))
    return pl.pallas_call(
        functools.partial(feed_backward_kernel, 768),
        grid=(count // block,),
        in_specs=[rows(width), rows(width), rows(hidden), rows(width), rows(1)]
        + [whole(x.shape) for x in (wo, wu, wd, g1)],
        out_specs=[rows(hidden), rows(width), rows(width), rows(width),
                   pl.BlockSpec((8, width), lambda i: (0, 0)), pl.BlockSpec((8, hidden), lambda i: (0, 0))],
        out_shape=[
            jax.ShapeDtypeStruct((count, hidden), bf16),
            jax.ShapeDtypeStruct((count, width), f32),
            jax.ShapeDtypeStruct((count, width), bf16),
            jax.ShapeDtypeStruct((count, width), bf16),
            jax.ShapeDtypeStruct((8, width), f32),
            jax.ShapeDtypeStruct((8, hidden), f32),
        ],
        compiler_params=pltpu.CompilerParams(vmem_limit_bytes=VMEM_LIMIT),
        cost_estimate=pl.CostEstimate(
            flops=2 * count * width * (width + 2 * hidden), bytes_accessed=40 * 2**20, transcendentals=0
        ),
        name="feed_backward",
    )(r2, feed, slope, n1, inv, wo, wu, wd, g1)


def bit_of(axis, k):
    return lax.bitwise_and(lax.shift_right_logical(lax.axis_index(axis), k), 1)


def swap(values, axis, k, size):
    return lax.ppermute(values, axis, [(i, i ^ (1 << k)) for i in range(size)])


def add_low(left, right):
    return (left.astype(f32) + right.astype(f32)).astype(bf16)


def part_of(values, index, count):
    size = values.shape[0] // count
    return lax.dynamic_slice_in_dim(values, index * size, size, 0)


def scatter_sum(values, halving, whole_sums):
    for axis, k, size in halving:
        bit = bit_of(axis, k)
        got = swap(part_of(values, 1 - bit, 2), axis, k, size)
        values = add_low(part_of(values, bit, 2), got)
    for axis, k, size in whole_sums:
        values = add_low(values, swap(values, axis, k, size))
    return values


def gather_back(values, halving):
    for axis, k, size in reversed(halving):
        first = bit_of(axis, k) == 0
        got = swap(values, axis, k, size)
        values = jnp.concatenate([jnp.where(first, values, got), jnp.where(first, got, values)], axis=0)
    return values


def on_device(
    sizes, tokens, segments, query_weight, query_bias, key_weight, value_weight, value_bias, out_weight, out_bias,
    first_gain, first_shift, up_weight, up_bias, down_weight, down_bias, second_gain, second_shift, cotangent,
):
    row_size, seq_size = sizes
    row_count, pos, width = tokens.shape
    groups = math.gcd(row_count, seq_size)
    subs = seq_size // groups
    if row_count != groups or subs != 2:
        raise ValueError("unsupported split")
    me = lax.axis_index("seq")
    group, sub = me // subs, lax.rem(me, subs)
    length = pos * seq_size
    half = length // 2
    local = width // subs

    def send_rows(values):
        pieces = [lax.dynamic_index_in_dim(values, group, 0, keepdims=False)]
        for s in range(1, groups):
            block = lax.dynamic_index_in_dim(values, lax.rem(group + s, groups), 0, keepdims=False)
            pieces.append(lax.ppermute(block, "seq", [(i, (i + s * subs) % seq_size) for i in range(seq_size)]))
        return pieces

    def return_rows(values):
        pieces = [values[:pos]]
        for s in range(1, groups):
            pieces.append(
                lax.ppermute(values[s * pos : (s + 1) * pos], "seq", [(i, (i - s * subs) % seq_size) for i in range(seq_size)])
            )
        rows = []
        for r in range(groups):
            picked = pieces[0]
            for s in range(1, groups):
                picked = jnp.where(lax.rem(group + s, groups) == r, pieces[s], picked)
            rows.append(picked)
        return jnp.stack(rows)

    def core_swap(values):
        return swap(values, "seq", 0, seq_size)

    token_pieces = send_rows(tokens)
    tok_half = jnp.concatenate(token_pieces, axis=0)
    tok_full = jnp.concatenate(token_pieces + [core_swap(piece) for piece in token_pieces], axis=0)
    cot_half = jnp.concatenate(send_rows(cotangent), axis=0)

    seg_row = lax.dynamic_index_in_dim(segments, group, 0, keepdims=False)
    middle = seg_row[length // 2]
    seg_pieces = []
    for u in range(subs):
        for s in range(groups):
            quarter = lax.rem(group + groups - s, groups) * subs + lax.rem(sub + u, subs)
            seg_pieces.append(lax.dynamic_slice_in_dim(seg_row, quarter * pos, pos, 0))
    seg_k = jnp.stack(seg_pieces)[None]
    seg_q = seg_k.reshape(length, 1)
    outside = jnp.where(seg_q == middle, 0.0, BLOCKED)
    slot = (jnp.arange(PAIR) % HEAD)[None, :]
    q_mark = jnp.where(slot == 0, 1.0, jnp.where(slot == 1, outside, 0.0)).astype(bf16)
    k_mark = jnp.where(slot == 0, outside, jnp.where(slot == 1, 1.0, 0.0)).astype(bf16)

    def columns(weight):
        return lax.dynamic_slice_in_dim(weight, sub * local, local, weight.ndim - 1)

    w_qkv = jnp.concatenate([columns(query_weight), columns(key_weight), columns(value_weight)], axis=1)
    b_qkv = jnp.concatenate([columns(query_bias), jnp.zeros((local,), f32), columns(value_bias)])
    qkv = (jnp.dot(tok_full, w_qkv, preferred_element_type=f32) + b_qkv).astype(bf16)
    ctx, prob, inv = attention_forward(qkv, q_mark, k_mark, seg_q, seg_k)
    ctx_got = core_swap(ctx[half:])
    ctx_own = ctx[:half]
    wo = jnp.roll(out_weight, -sub * local, axis=0)
    line = lambda vec: vec.reshape(1, -1)
    out, act, slope, r2, feed, n1, hid, inv1, sums_two = feed_forward(
        ctx_own, ctx_got, tok_half, cot_half, wo, up_weight, down_weight, line(out_bias), line(first_gain),
        line(first_shift), line(up_bias), line(down_bias), line(second_gain), line(second_shift),
    )
    output = return_rows(out)

    x_bit, y_bit = ("seq", 1, seq_size), ("rows", 0, row_size)
    row_bits = row_size.bit_length() - 1
    z_bits = [("rows", k, row_size) for k in range(1, min(3, row_bits))]
    more = [("rows", k, row_size) for k in range(3, row_bits)]
    x_first, y_first = [x_bit, y_bit] + z_bits, [y_bit, x_bit] + z_bits

    def total_of(values, order):
        return gather_back(scatter_sum(values, order, more), order)

    def over_rows(left, right):
        return dot(left, right, 0, 0).astype(bf16)

    def cols_of(values, index):
        size = values.shape[1] // 2
        return lax.dynamic_slice_in_dim(values, index * size, size, 1)

    def core_sum(make):
        got = core_swap(make(1 - sub))
        return add_low(make(sub), got)

    def both_halves(values):
        got = core_swap(values)
        first = sub == 0
        return jnp.where(first, values, got), jnp.where(first, got, values)

    down = core_sum(lambda i: over_rows(cols_of(act, i), feed))
    down = jnp.concatenate([total_of(down[:, :local], x_first), total_of(down[:, local:], y_first)], axis=1)
    downweight_grad = jnp.concatenate(both_halves(down), axis=0).astype(f32)

    pre, r1, branch, dctx, sums_one, sums_up = feed_backward(r2, feed, slope, n1, inv1, wo, up_weight, down_weight, line(first_gain))
    dctx_got = core_swap(dctx[:, local:])
    grad = jnp.concatenate([dctx[:, :local], dctx_got], axis=0)

    up = core_sum(lambda i: over_rows(hid, cols_of(pre, i)))
    up = jnp.concatenate([total_of(up[:, :width], x_first), total_of(up[:, width:], y_first)], axis=1)
    upweight_grad = jnp.concatenate(both_halves(up), axis=1).astype(f32)

    ctx_both = jnp.concatenate([ctx_own, ctx_got], axis=1)
    outw = core_sum(lambda i: over_rows(ctx_both, cols_of(branch, i)))

    del outw

    def out_half(i):
        rows = over_rows(ctx_both, cols_of(branch, i))
        return jnp.roll(rows, sub * local, axis=0)

    outw = total_of(core_sum(out_half), y_first)
    outweight_grad = jnp.concatenate(both_halves(outw), axis=1).astype(f32)

    grads, dqkv = [], []
    for p in range(local // PAIR):
        dq, dk, dv = attention_backward(p, grad, ctx, inv, qkv, prob)
        dqkv.append((dq, dk, dv))
        wide = jnp.concatenate([dq, dk, dv], axis=1)
        summed = total_of(over_rows(tok_full, wide), x_first if p == 1 else y_first)
        grads.append(both_halves(summed))
    qkv_grads = []
    for i in range(3):
        cols = slice(i * PAIR, (i + 1) * PAIR)
        qkv_grads.append(
            jnp.concatenate([g[0][:, cols] for g in grads] + [g[1][:, cols] for g in grads], axis=1).astype(f32)
        )
    dall = jnp.concatenate([d[i] for i in range(3) for d in dqkv], axis=1)
    share = dot(dall, w_qkv, 1, 1)
    share_got = core_swap(share[half:].astype(bf16))
    in_half = r1 + share[:half] + share_got.astype(f32)
    kept = in_half[:pos]
    pieces = [kept]
    for s in range(1, groups):
        low = in_half[s * pos : (s + 1) * pos].astype(bf16)
        pieces.append(
            lax.ppermute(low, "seq", [(i, (i - s * subs) % seq_size) for i in range(seq_size)]).astype(f32)
        )
    in_rows = []
    for r in range(groups):
        picked = pieces[0]
        for s in range(1, groups):
            picked = jnp.where(lax.rem(group + s, groups) == r, pieces[s], picked)
        in_rows.append(picked)
    input_grad = jnp.stack(in_rows)

    bias_sums = jnp.sum(dall.astype(f32), axis=0)
    place = lambda part: lax.dynamic_update_slice_in_dim(jnp.zeros((width,), f32), part, sub * local, 0)
    small = lax.psum(
        jnp.concatenate(
            [
                sums_two[0], sums_two[1], sums_two[2], sums_one[0], sums_one[1], sums_one[2], sums_up[0],
                place(bias_sums[:local]), place(bias_sums[2 * local :]),
            ]
        ),
        ("rows", "seq"),
    )
    gain_two, shift_two, down_bias_grad, gain_one, shift_one, out_bias_grad = [
        small[i * width : (i + 1) * width] for i in range(6)
    ]
    hidden = up_bias.shape[0]
    up_bias_grad = small[6 * width : 6 * width + hidden]
    query_bias_grad = small[6 * width + hidden : 7 * width + hidden]
    value_bias_grad = small[7 * width + hidden :]
    return (
        output, input_grad, qkv_grads[0], query_bias_grad, qkv_grads[1], qkv_grads[2], value_bias_grad, outweight_grad,
        out_bias_grad, gain_one, shift_one, upweight_grad, up_bias_grad, downweight_grad, down_bias_grad, gain_two, shift_two,
    )


def solution(mesh):
    split = P("rows", "seq", None)
    return jax.shard_map(
        functools.partial(on_device, (mesh.shape["rows"], mesh.shape["seq"])),
        mesh=mesh,
        in_specs=(split, P("rows", None)) + (P(),) * 15 + (split,),
        out_specs=(split, split) + (P(),) * 15,
        check_vma=False,
    )
```

time: 1890 us -> 623 us (0.33)
  waiting for transfers between devices: 930 us -> 157 us
  local copies, waits for them, and re-layouts: 422 us -> 48.7 us
  matrix products: 373 us -> 43.1 us
  Pallas kernels: 0 us -> 158 us
  starting transfers between devices: 0.42 us -> 97.3 us
  other arithmetic: 125 us -> 70.1 us
  blocking collectives: 0 us -> 40.4 us
    unnamed x8 -> x0, waiting for transfers between devices: 855 us -> none
    dot_general x24 -> x11, matrix products: 373 us -> 43.1 us  [the longest x10 35.3 us: dot(): lax.dot_general(left, right, (((over_left,), (over_right,)), ((), ())), p...]
    unnamed x135 -> x128, local copies, waits for them, and re-layouts: 274 us -> 19.7 us
    pallas_call x0 -> x6, Pallas kernels: none -> 158 us  [the longest x3 62.5 us: attention_backward(): pl.pallas_call(functools.partial(attention_backward_kernel, chunk), grid=...]
    ppermute x0 -> x82, waiting for transfers between devices: none -> 157 us  [the longest x78 144 us: swap(): return lax.ppermute(values, axis, [(i, i ^ 1 << k) for i in range(size)])]
    ppermute x0 -> x82, starting transfers between devices: none -> 97.3 us  [the longest x78 91 us: swap(): return lax.ppermute(values, axis, [(i, i ^ 1 << k) for i in range(size)])]
    reshape x10 -> x6, local copies, waits for them, and re-layouts: 65.5 us -> 4.85 us  [on_device(): line = lambda vec: vec.reshape(1, -1)]
    convert_element_type x2 -> x42, other arithmetic: 80.2 us -> 26.3 us  [the longest x35 9.15 us: add_low(): return (left.astype(f32) + right.astype(f32)).astype(bf16)]
  transfers between devices with their start and end apart: 6 -> 82, of which waited for: 4 -> 46; matrix products, arithmetic and copies ran while one was open for 14% -> 22% of each run, Pallas kernels for 0% -> 21%
where the time goes in v1:
time: 623 us; the launch traced here: 617 us
  Pallas kernels  158 us (25%)
  waiting for transfers between devices  157 us (25%)
  starting transfers between devices  97.3 us (16%)
  other arithmetic  70.1 us (11%)
  local copies, waits for them, and re-layouts  48.7 us (8%)
  matrix products  43.1 us (7%)
  blocking collectives  40.4 us (6%)
    ppermute x78, waiting for transfers between devices, swap(): return lax.ppermute(values, axis, [(i, i ^ 1 << k) for i in range(size)])  144 us
    ppermute x78, starting transfers between devices, swap(): return lax.ppermute(values, axis, [(i, i ^ 1 << k) for i in range(size)])  91 us
    pallas_call x3, Pallas kernels, attention_backward(): pl.pallas_call(functools.partial(attention_backward_kernel, chunk), grid=...  62.5 us
    pallas_call x1, Pallas kernels, attention_forward(): pl.pallas_call(functools.partial(attention_forward_kernel, block, piece),...  47.7 us
    psum x1, blocking collectives, on_device(): lax.psum(jnp.concatenate([sums_two[0], sums_two[1], sums_two[2], sums_one...  40.4 us
    dot_general x10, matrix products, dot(): lax.dot_general(left, right, (((over_left,), (over_right,)), ((), ())), p...  35.3 us
    pallas_call x1, Pallas kernels, feed_forward(): pl.pallas_call(functools.partial(feed_forward_kernel, 768), grid=(count /...  26.6 us
    pallas_call x1, Pallas kernels, feed_backward(): pl.pallas_call(functools.partial(feed_backward_kernel, 768), grid=(count...  20.9 us
  transfers between devices with their start and end apart: 82, of which 46 were waited for; matrix products, arithmetic and copies ran while one was open for 22% of the time, Pallas kernels for 21%

profile of v1, /device:TPU:0, one launch (start us, length us, event | category | flops | bytes accessed | tf_op | source)
XLA Modules:
  0.0 616.8 jit_solution(12357277885909124313)
XLA Ops:
  3.2 2.9 collective-permute-start
  11.9 12.8 %collective-permute-done = bf16[512,768]{1,0:T(8,128)(2,1)S(1)} collective-permute-done((bf16[512,768]{1,0:T(8,128)(2,1)}, bf16[512,768]{1,0:T(8,128)(2,1)S(1)}, u32[]{:S(2)}, u32[]{:S(2)}) %collective-permute-start) | collective-permute-done | bytes 786464 | tf_op jit(solution)/shard_map/ppermute | solution.py:392
  29.7 7.9 %add_convert_fusion.q_ref.k_ref.v_ref = bf16[2048,1152]{1,0:T(8,128)(2,1)} fusion(f32[1152]{0:T(1024)S(1)} %copy-done.35, bf16[768,384]{1,0:T(8,128)(2,1)S(1)} %get-tuple-element.206, bf16[768,384]{1,0:T(8,128)(2,1)S(1)} %get-tuple-element.207, bf16[768,384]{1,0:T(8,128)(2,1)S(1)} %constant_dynamic-slice_fusion.34, ...), kind=kOutput, calls=%fused_computation.1 | convolution fusion | flops 3646488576 | bytes 9638400 | tf_op jit(solution)/shard_map/dot_general | solution.py:436
  37.6 47.7 %attention_forward.1 = (bf16[2048,384]{1,0:T(8,128)(2,1)}, bf16[6,2048,2048]{2,1,0:T(8,128)(2,1)}, f32[2048,384]{1,0:T(8,128)}) custom-call(bf16[2048,1152]{1,0:T(8,128)(2,1)} %add_convert_fusion.q_ref.k_ref.v_ref, bf16[2048,1152]{1,0:T(8,128)(2,1)} %add_convert_fusion.q_ref.k_ref.v_ref, bf16[2048,1152]{1,0:T(8,128)(2,1)} %add_convert_fusion.q_ref.k_ref.v_ref, ...), custom_call_target="tpu_custom_call" | custom-call | flops 25769803776 | bytes 50331648 | tf_op jit(solution)/shard_map/attention_forward/pallas_call | solution.py:71
  85.3 2.8 fusion.58
  93.4 2.9 fusion.34.wo_ref
  100.0 26.6 %feed_forward.1 = (bf16[1024,768]{1,0:T(8,128)(2,1)}, bf16[1024,3072]{1,0:T(8,128)(2,1)}, bf16[1024,3072]{1,0:T(8,128)(2,1)}, f32[1024,768]{1,0:T(8,128)}, bf16[...) custom-call(bf16[1024,384]{1,0:T(8,128)(2,1)} %get-tuple-element.95., ...), custom_call_target="tpu_custom_call" | custom-call | flops 10871635968 | bytes 41943040 | tf_op jit(solution)/shard_map/feed_forward/pallas_call | solution.py:284
  130.8 20.9 %feed_backward.1 = (bf16[1024,3072]{1,0:T(8,128)(2,1)}, f32[1024,768]{1,0:T(8,128)}, bf16[1024,768]{1,0:T(8,128)(2,1)}, bf16[1024,768]{1,0:T(8,128)(2,1)}, f32[8,768]{1,0:T(8,128)}, /*index=5*/f32[8,3072]{1,0:T(8,128)}) custom-call(f32[1024,768]{1,0:T(8,128)} %get-tuple-element.47.r2_ref, bf16[1024,768]{1,0:T(8,128)(2,1)} %get-tuple-element.48.feed_ref, ...), custom_call_target="tpu_custom_call" | custom-call | flops 10871635968 | bytes 41943040 | tf_op jit(solution)/shard_map/feed_backward/pallas_call | solution.py:314
  160.4 4.0 convolution_convert_fusion.2
  164.4 4.0 convolution_convert_fusion.3
  168.4 4.0 convolution_convert_fusion
  184.1 4.1 convolution_convert_fusion.1
  193.2 20.6 %attention_backward.3 = (bf16[2048,128]{1,0:T(8,128)(2,1)}, bf16[2048,128]{1,0:T(8,128)(2,1)}, bf16[2048,128]{1,0:T(8,128)(2,1)}) custom-call(bf16[2048,384]{1,0:T(8,128)(2,1)} %pad_maximum_fusion.6.do_ref, bf16[2048,384]{1,0:T(8,128)(2,1)} %get-tuple-element.45.ctx_ref, f32[2048,384]{1,0:T(8,128)} %get-tuple-element.54.inv_ref, ...), custom_call_target="tpu_custom_call" | custom-call | flops 17179869184 | bytes 16777216 | tf_op jit(solution)/shard_map/attention_backward/pallas_call | solution.py:161
  213.8 20.7 %attention_backward.4 = (bf16[2048,128]{1,0:T(8,128)(2,1)}, bf16[2048,128]{1,0:T(8,128)(2,1)}, bf16[2048,128]{1,0:T(8,128)(2,1)}) custom-call(bf16[2048,384]{1,0:T(8,128)(2,1)} %pad_maximum_fusion.6.do_ref, bf16[2048,384]{1,0:T(8,128)(2,1)} %get-tuple-element.45.ctx_ref, f32[2048,384]{1,0:T(8,128)} %get-tuple-element.54.inv_ref, ...), custom_call_target="tpu_custom_call" | custom-call | flops 17179869184 | bytes 16777216 | tf_op jit(solution)/shard_map/attention_backward/pallas_call | solution.py:161
  234.5 21.1 %attention_backward.5 = (bf16[2048,128]{1,0:T(8,128)(2,1)}, bf16[2048,128]{1,0:T(8,128)(2,1)}, bf16[2048,128]{1,0:T(8,128)(2,1)}) custom-call(bf16[2048,384]{1,0:T(8,128)(2,1)} %pad_maximum_fusion.6.do_ref, bf16[2048,384]{1,0:T(8,128)(2,1)} %get-tuple-element.45.ctx_ref, f32[2048,384]{1,0:T(8,128)} %get-tuple-element.54.inv_ref, ...), custom_call_target="tpu_custom_call" | custom-call | flops 17179869184 | bytes 16777216 | tf_op jit(solution)/shard_map/attention_backward/pallas_call | solution.py:161
  258.7 4.3 fusion.37
  266.0 3.2 fusion.31
  270.8 3.2 fusion.25
  277.5 40.4 %psum.7 = f32[9216]{0:T(1024)} all-reduce(f32[9216]{0:T(1024)} %constant_dynamic-update-slice_fusion.11), channel_id=1, replica_groups=mesh['rows'=8,'seq'=4] {'rows','seq'}, use_global_device_ids=true, to_apply=%region_1.2 | all-reduce | flops 9216 | bytes 73728 | tf_op jit(solution)/shard_map/psum | solution.py:531
  319.3 4.0 fusion.28
  330.7 3.7 collective-permute-done.38
  336.7 4.7 collective-permute-done.27
  348.2 2.9 collective-permute-done.40
  353.2 2.9 collective-permute-done.41
  357.9 3.4 collective-permute-done.19
  362.9 2.6 collective-permute-start.11
  374.6 2.8 collective-permute-done.12
  379.5 2.8 collective-permute-done.21
  384.3 2.9 collective-permute-done.30
  389.6 2.5 collective-permute-done.13
  412.1 4.0 collective-permute-done.15
  417.2 4.0 collective-permute-done.33
  422.7 3.7 collective-permute-done.24
  429.2 3.9 collective-permute-done.16
  434.9 4.9 collective-permute-done.34
  458.6 7.4 %collective-permute-done.55 = bf16[384,768]{1,0:T(8,128)(2,1)S(1)} collective-permute-done((bf16[384,768]{1,0:T(8,128)(2,1)S(1)}, bf16[384,768]{1,0:T(8,128)(2,1)S(1)}, u32[]{:S(2)}, u32[]{:S(2)}) %collective-permute-start.55) | collective-permute-done | bytes 589856 | tf_op jit(solution)/shard_map/ppermute | solution.py:342
  467.3 11.9 %collective-permute-done.47 = bf16[384,768]{1,0:T(8,128)(2,1)S(1)} collective-permute-done((bf16[384,768]{1,0:T(8,128)(2,1)S(1)}, bf16[384,768]{1,0:T(8,128)(2,1)S(1)}, u32[]{:S(2)}, u32[]{:S(2)}) %collective-permute-start.47) | collective-permute-done | bytes 589856 | tf_op jit(solution)/shard_map/ppermute | solution.py:342
  482.3 9.5 %collective-permute-done.65 = bf16[768,384]{1,0:T(8,128)(2,1)S(1)} collective-permute-done((bf16[768,384]{1,0:T(8,128)(2,1)S(1)}, bf16[768,384]{1,0:T(8,128)(2,1)S(1)}, u32[]{:S(2)}, u32[]{:S(2)}) %collective-permute-start.65) | collective-permute-done | bytes 589856 | tf_op jit(solution)/shard_map/ppermute | solution.py:342
  493.5 4.7 collective-permute-done.56
  500.5 3.1 collective-permute-done.74
  509.3 4.7 collective-permute-done.75
  520.3 4.9 collective-permute-done.76
  557.7 10.8 %collective-permute-done.62 = bf16[384,768]{1,0:T(8,128)(2,1)S(1)} collective-permute-done((bf16[384,768]{1,0:T(8,128)(2,1)S(1)}, bf16[384,768]{1,0:T(8,128)(2,1)S(1)}, u32[]{:S(2)}, u32[]{:S(2)}) %collective-permute-start.62) | collective-permute-done | bytes 589856 | tf_op jit(solution)/shard_map/ppermute | solution.py:342
  569.6 9.6 %collective-permute-done.80 = bf16[768,384]{1,0:T(8,128)(2,1)S(1)} collective-permute-done((bf16[768,384]{1,0:T(8,128)(2,1)S(1)}, bf16[768,384]{1,0:T(8,128)(2,1)S(1)}, u32[]{:S(2)}, u32[]{:S(2)}) %collective-permute-start.80) | collective-permute-done | bytes 589856 | tf_op jit(solution)/shard_map/ppermute | solution.py:342
  587.2 10.2 %broadcast_select_fusion.3 = (bf16[768,1536]{1,0:T(8,128)(2,1)S(1)}, bf16[768,1536]{1,0:T(8,128)(2,1)S(1)}) fusion(bf16[768,1536]{1,0:T(8,128)(2,1)S(1)} %collective-permute-done.63, pred[]{:T(512)S(6)} %eq.105, bf16[384,768]{1,0:T(8,128)(2,1)S(1)} %get-tuple-element.105, bf16[384,768]{1,0:T(8,128)(2,1)S(1)} %get-tuple-element.104, ...), kind=kLoop, calls=%fused_computation.26 | loop fusion | flops 11796480 | bytes 9437185 | tf_op jit(solution)/shard_map/jit(_where)/select_n | solution.py:471
  597.4 5.0 maximum_convert_fusion
  602.5 9.4 %broadcast_select_fusion.1 = (bf16[1536,768]{1,0:T(8,128)(2,1)S(1)}, bf16[1536,768]{1,0:T(8,128)(2,1)S(1)}) fusion(bf16[1536,768]{1,0:T(8,128)(2,1)S(1)} %collective-permute-done.81, pred[]{:T(512)S(6)} %eq.105, bf16[768,384]{1,0:T(8,128)(2,1)S(1)} %get-tuple-element.101, bf16[768,384]{1,0:T(8,128)(2,1)S(1)} %get-tuple-element.100, ...), kind=kLoop, calls=%fused_computation.24 | loop fusion | flops 11796480 | bytes 9437185 | tf_op jit(solution)/shard_map/jit(_where)/select_n | solution.py:471
  611.9 4.5 maximum_convert_fusion.1
  (457 shorter events, 208.3 us)
Async XLA Ops:
  3.2 21.5 %collective-permute-start = (bf16[512,768]{1,0:T(8,128)(2,1)}, bf16[512,768]{1,0:T(8,128)(2,1)S(1)}, u32[]{:S(2)}, u32[]{:S(2)}) collective-permute-start(bf16[512,768]{1,0:T(8,128)(2,1)} %get-tuple-element.97), channel_id=1, source_target_pairs={{0,2},{1,3},{2,0},{3,1},{4,6},{5,7},{6,4},{7,5},{8,10},{9,11},{10,... | collective-permute-start | bytes 2359304 | tf_op jit(solution)/shard_map/ppermute | solution.py:392
  6.2 23.5 %collective-permute-start.1 = (bf16[512,768]{1,0:T(8,128)(2,1)S(1)}, bf16[512,768]{1,0:T(8,128)(2,1)}, u32[]{:S(2)}, u32[]{:S(2)}) collective-permute-start(bf16[512,768]{1,0:T(8,128)(2,1)S(1)} %get-tuple-element.96), channel_id=1, source_target_pairs={{0,1},{1,0},{2,3},{3,2},{4,5},{5,4},{6,7},{7,6},{8,9},{9,8},{10,11... | collective-permute-start | bytes 2359304 | tf_op jit(solution)/shard_map/ppermute | solution.py:342
  7.2 90.5 %collective-permute-start.4 = (bf16[512,768]{1,0:T(8,128)(2,1)}, bf16[512,768]{1,0:T(8,128)(2,1)}, u32[]{:S(2)}, u32[]{:S(2)}) collective-permute-start(bf16[512,768]{1,0:T(8,128)(2,1)} %get-tuple-element.93), channel_id=1, source_target_pairs={{0,2},{1,3},{2,0},{3,1},{4,6},{5,7},{6,4},{7,5},{8,10},{9,11},{10,... | collective-permute-start | bytes 2359304 | tf_op jit(solution)/shard_map/ppermute | solution.py:392
  88.1 11.9 %collective-permute-start.3 = (bf16[1024,384]{1,0:T(8,128)(2,1)}, bf16[1024,384]{1,0:T(8,128)(2,1)}, u32[]{:S(2)}, u32[]{:S(2)}) collective-permute-start(bf16[1024,384]{1,0:T(8,128)(2,1)} %get-tuple-element.94), channel_id=1, source_target_pairs={{0,1},{1,0},{2,3},{3,2},{4,5},{5,4},{6,7},{7,6},{8,9},{9,8},{10,11... | collective-permute-start | bytes 2359304 | tf_op jit(solution)/shard_map/ppermute | solution.py:342
  128.7 195.3 %collective-permute-start.5 = (bf16[512,768]{1,0:T(8,128)(2,1)}, bf16[512,768]{1,0:T(8,128)(2,1)}, u32[]{:S(2)}, u32[]{:S(2)}) collective-permute-start(bf16[512,768]{1,0:T(8,128)(2,1)} %slice.159), channel_id=1, source_target_pairs={{0,2},{1,3},{2,0},{3,1},{4,6},{5,7},{6,4},{7,5},{8,10},{9,11},{10,... | collective-permute-start | bytes 2359304 | tf_op jit(solution)/shard_map/ppermute | solution.py:399
  153.4 38.4 %collective-permute-start.6 = (bf16[1024,384]{1,0:T(8,128)(2,1)S(1)}, bf16[1024,384]{1,0:T(8,128)(2,1)S(1)}, u32[]{:S(2)}, u32[]{:S(2)}) collective-permute-start(bf16[1024,384]{1,0:T(8,128)(2,1)S(1)} %get-tuple-element.91), channel_id=1, source_target_pairs={{0,1},{1,0},{2,3},{3,2},{4,5},{5,4},{6,7},{7,6},{8,9},{9,8},{10,11... | collective-permute-start | bytes 2359304 | tf_op jit(solution)/shard_map/ppermute | solution.py:342
  159.8 28.4 %collective-permute-start.36 = (bf16[768,384]{1,0:T(8,128)(2,1)S(1)}, bf16[768,384]{1,0:T(8,128)(2,1)S(1)}, u32[]{:S(2)}, u32[]{:S(2)}) collective-permute-start(bf16[768,384]{1,0:T(8,128)(2,1)S(1)} %fusion.38), channel_id=1, source_target_pairs={{0,1},{1,0},{2,3},{3,2},{4,5},{5,4},{6,7},{7,6},{8,9},{9,8},{10,11... | collective-permute-start | bytes 1769480 | tf_op jit(solution)/shard_map/ppermute | solution.py:342
  164.4 281.7 %collective-permute-start.46 = (bf16[768,1536]{1,0:T(8,128)(2,1)}, bf16[768,1536]{1,0:T(8,128)(2,1)}, u32[]{:S(2)}, u32[]{:S(2)}) collective-permute-start(bf16[768,1536]{1,0:T(8,128)(2,1)} %convolution_convert_fusion.2), channel_id=1, source_target_pairs={{0,1},{1,0},{2,3},{3,2},{4,5},{5,4},{6,7},{7,6},{8,9},{9,8},{10,11... | collective-permute-start | bytes 7077896 | tf_op jit(solution)/shard_map/ppermute | solution.py:342
  172.4 277.4 %collective-permute-start.64 = (bf16[1536,768]{1,0:T(8,128)(2,1)}, bf16[1536,768]{1,0:T(8,128)(2,1)}, u32[]{:S(2)}, u32[]{:S(2)}) collective-permute-start(bf16[1536,768]{1,0:T(8,128)(2,1)} %convolution_convert_fusion), channel_id=1, source_target_pairs={{0,1},{1,0},{2,3},{3,2},{4,5},{5,4},{6,7},{7,6},{8,9},{9,8},{10,11... | collective-permute-start | bytes 7077896 | tf_op jit(solution)/shard_map/ppermute | solution.py:342
  190.3 137.3 %collective-permute-start.37 = (bf16[384,384]{1,0:T(8,128)(2,1)}, bf16[384,384]{1,0:T(8,128)(2,1)}, u32[]{:S(2)}, u32[]{:S(2)}) collective-permute-start(bf16[384,384]{1,0:T(8,128)(2,1)} %constant_dynamic-slice_fusion.19), channel_id=1, source_target_pairs={{0,4},{4,0},{8,12},{12,8},{16,20},{20,16},{24,28},{28,24},{1,5},{5... | collective-permute-start | bytes 884744 | tf_op jit(solution)/shard_map/ppermute | solution.py:342
  263.9 178.6 %collective-permute-start.7 = (bf16[1024,768]{1,0:T(8,128)(2,1)S(1)}, bf16[1024,768]{1,0:T(8,128)(2,1)}, u32[]{:S(2)}, u32[]{:S(2)}) collective-permute-start(bf16[1024,768]{1,0:T(8,128)(2,1)S(1)} %slice.279), channel_id=1, source_target_pairs={{0,1},{1,0},{2,3},{3,2},{4,5},{5,4},{6,7},{7,6},{8,9},{9,8},{10,11... | collective-permute-start | bytes 4718600 | tf_op jit(solution)/shard_map/ppermute | solution.py:342
  324.0 10.6 %collective-permute-start.9 = (bf16[384,384]{1,0:T(8,128)(2,1)S(1)}, bf16[384,384]{1,0:T(8,128)(2,1)S(1)}, u32[]{:S(2)}, u32[]{:S(2)}) collective-permute-start(bf16[384,384]{1,0:T(8,128)(2,1)S(1)} %copy-done.33), channel_id=1, source_target_pairs={{0,4},{4,0},{8,12},{12,8},{16,20},{20,16},{24,28},{28,24},{1,5},{5... | collective-permute-start | bytes 884744 | tf_op jit(solution)/shard_map/ppermute | solution.py:342
  343.0 14.6 %collective-permute-start.10 = (bf16[192,384]{1,0:T(8,128)(2,1)S(1)}, bf16[192,384]{1,0:T(8,128)(2,1)S(1)}, u32[]{:S(2)}, u32[]{:S(2)}) collective-permute-start(bf16[192,384]{1,0:T(8,128)(2,1)S(1)} %constant_dynamic-slice_fusion.30), channel_id=1, source_target_pairs={{0,2},{1,3},{2,0},{3,1},{4,6},{5,7},{6,4},{7,5},{8,10},{9,11},{10,... | collective-permute-start | bytes 442376 | tf_op jit(solution)/shard_map/ppermute | solution.py:342
  370.3 34.0 %collective-permute-start.43 = (bf16[192,384]{1,0:T(8,128)(2,1)S(1)}, bf16[192,384]{1,0:T(8,128)(2,1)S(1)}, u32[]{:S(2)}, u32[]{:S(2)}) collective-permute-start(bf16[192,384]{1,0:T(8,128)(2,1)S(1)} %pad_maximum_fusion.31), channel_id=1, source_target_pairs={{0,2},{1,3},{2,0},{3,1},{4,6},{5,7},{6,4},{7,5},{8,10},{9,11},{10,... | collective-permute-start | bytes 442376 | tf_op jit(solution)/shard_map/ppermute | solution.py:342
  408.7 19.2 %collective-permute-start.44 = (bf16[384,384]{1,0:T(8,128)(2,1)S(1)}, bf16[384,384]{1,0:T(8,128)(2,1)S(1)}, u32[]{:S(2)}, u32[]{:S(2)}) collective-permute-start(bf16[384,384]{1,0:T(8,128)(2,1)S(1)} %pad_maximum_fusion.23), channel_id=1, source_target_pairs={{0,4},{4,0},{8,12},{12,8},{16,20},{20,16},{24,28},{28,24},{1,5},{5... | collective-permute-start | bytes 884744 | tf_op jit(solution)/shard_map/ppermute | solution.py:342
  439.8 14.2 %collective-permute-start.17 = (bf16[768,384]{1,0:T(8,128)(2,1)S(1)}, bf16[768,384]{1,0:T(8,128)(2,1)S(1)}, u32[]{:S(2)}, u32[]{:S(2)}) collective-permute-start(bf16[768,384]{1,0:T(8,128)(2,1)S(1)} %pad_maximum_fusion.12), channel_id=1, source_target_pairs={{0,1},{1,0},{2,3},{3,2},{4,5},{5,4},{6,7},{7,6},{8,9},{9,8},{10,11... | collective-permute-start | bytes 1769480 | tf_op jit(solution)/shard_map/ppermute | solution.py:342
  440.1 15.2 %collective-permute-start.26 = (bf16[768,384]{1,0:T(8,128)(2,1)S(1)}, bf16[768,384]{1,0:T(8,128)(2,1)S(1)}, u32[]{:S(2)}, u32[]{:S(2)}) collective-permute-start(bf16[768,384]{1,0:T(8,128)(2,1)S(1)} %pad_maximum_fusion.13), channel_id=1, source_target_pairs={{0,1},{1,0},{2,3},{3,2},{4,5},{5,4},{6,7},{7,6},{8,9},{9,8},{10,11... | collective-permute-start | bytes 1769480 | tf_op jit(solution)/shard_map/ppermute | solution.py:342
  442.5 14.6 %collective-permute-start.35 = (bf16[768,384]{1,0:T(8,128)(2,1)S(1)}, bf16[768,384]{1,0:T(8,128)(2,1)S(1)}, u32[]{:S(2)}, u32[]{:S(2)}) collective-permute-start(bf16[768,384]{1,0:T(8,128)(2,1)S(1)} %pad_maximum_fusion.14), channel_id=1, source_target_pairs={{0,1},{1,0},{2,3},{3,2},{4,5},{5,4},{6,7},{7,6},{8,9},{9,8},{10,11... | collective-permute-start | bytes 1769480 | tf_op jit(solution)/shard_map/ppermute | solution.py:342
  446.1 139.0 %collective-permute-start.8 = (bf16[512,768]{1,0:T(8,128)(2,1)S(1)}, bf16[512,768]{1,0:T(8,128)(2,1)S(1)}, u32[]{:S(2)}, u32[]{:S(2)}) collective-permute-start(bf16[512,768]{1,0:T(8,128)(2,1)S(1)} %slice.280), channel_id=1, source_target_pairs={{0,2},{1,3},{2,0},{3,1},{4,6},{5,7},{6,4},{7,5},{8,10},{9,11},{10,... | collective-permute-start | bytes 2359304 | tf_op jit(solution)/shard_map/ppermute | solution.py:519
  449.8 16.3 %collective-permute-start.55 = (bf16[384,768]{1,0:T(8,128)(2,1)S(1)}, bf16[384,768]{1,0:T(8,128)(2,1)S(1)}, u32[]{:S(2)}, u32[]{:S(2)}) collective-permute-start(bf16[384,768]{1,0:T(8,128)(2,1)S(1)} %constant_dynamic-slice_fusion.11), channel_id=1, source_target_pairs={{0,4},{4,0},{8,12},{12,8},{16,20},{20,16},{24,28},{28,24},{1,5},{5... | collective-permute-start | bytes 1769480 | tf_op jit(solution)/shard_map/ppermute | solution.py:342
  454.0 25.1 %collective-permute-start.47 = (bf16[384,768]{1,0:T(8,128)(2,1)S(1)}, bf16[384,768]{1,0:T(8,128)(2,1)S(1)}, u32[]{:S(2)}, u32[]{:S(2)}) collective-permute-start(bf16[384,768]{1,0:T(8,128)(2,1)S(1)} %constant_dynamic-slice_fusion.15), channel_id=1, source_target_pairs={{0,2},{1,3},{2,0},{3,1},{4,6},{5,7},{6,4},{7,5},{8,10},{9,11},{10,... | collective-permute-start | bytes 1769480 | tf_op jit(solution)/shard_map/ppermute | solution.py:342
  455.3 25.5 %collective-permute-start.73 = (bf16[768,384]{1,0:T(8,128)(2,1)S(1)}, bf16[768,384]{1,0:T(8,128)(2,1)S(1)}, u32[]{:S(2)}, u32[]{:S(2)}) collective-permute-start(bf16[768,384]{1,0:T(8,128)(2,1)S(1)} %constant_dynamic-slice_fusion.3), channel_id=1, source_target_pairs={{0,4},{4,0},{8,12},{12,8},{16,20},{20,16},{24,28},{28,24},{1,5},{5... | collective-permute-start | bytes 1769480 | tf_op jit(solution)/shard_map/ppermute | solution.py:342
  457.1 34.7 %collective-permute-start.65 = (bf16[768,384]{1,0:T(8,128)(2,1)S(1)}, bf16[768,384]{1,0:T(8,128)(2,1)S(1)}, u32[]{:S(2)}, u32[]{:S(2)}) collective-permute-start(bf16[768,384]{1,0:T(8,128)(2,1)S(1)} %constant_dynamic-slice_fusion.7), channel_id=1, source_target_pairs={{0,2},{1,3},{2,0},{3,1},{4,6},{5,7},{6,4},{7,5},{8,10},{9,11},{10,... | collective-permute-start | bytes 1769480 | tf_op jit(solution)/shard_map/ppermute | solution.py:342
  466.2 31.9 %collective-permute-start.56 = (bf16[192,768]{1,0:T(8,128)(2,1)S(1)}, bf16[192,768]{1,0:T(8,128)(2,1)S(1)}, u32[]{:S(2)}, u32[]{:S(2)}) collective-permute-start(bf16[192,768]{1,0:T(8,128)(2,1)S(1)} %constant_dynamic-slice_fusion.10), channel_id=1, source_target_pairs={{0,2},{1,3},{2,0},{3,1},{4,6},{5,7},{6,4},{7,5},{8,10},{9,11},{10,... | collective-permute-start | bytes 884744 | tf_op jit(solution)/shard_map/ppermute | solution.py:342
  479.4 21.0 %collective-permute-start.48 = (bf16[192,768]{1,0:T(8,128)(2,1)S(1)}, bf16[192,768]{1,0:T(8,128)(2,1)S(1)}, u32[]{:S(2)}, u32[]{:S(2)}) collective-permute-start(bf16[192,768]{1,0:T(8,128)(2,1)S(1)} %constant_dynamic-slice_fusion.14), channel_id=1, source_target_pairs={{0,4},{4,0},{8,12},{12,8},{16,20},{20,16},{24,28},{28,24},{1,5},{5... | collective-permute-start | bytes 884744 | tf_op jit(solution)/shard_map/ppermute | solution.py:342
  481.3 22.4 %collective-permute-start.74 = (bf16[384,384]{1,0:T(8,128)(2,1)S(1)}, bf16[384,384]{1,0:T(8,128)(2,1)S(1)}, u32[]{:S(2)}, u32[]{:S(2)}) collective-permute-start(bf16[384,384]{1,0:T(8,128)(2,1)S(1)} %constant_dynamic-slice_fusion.2), channel_id=1, source_target_pairs={{0,2},{1,3},{2,0},{3,1},{4,6},{5,7},{6,4},{7,5},{8,10},{9,11},{10,... | collective-permute-start | bytes 884744 | tf_op jit(solution)/shard_map/ppermute | solution.py:342
  492.0 13.8 %collective-permute-start.66 = (bf16[384,384]{1,0:T(8,128)(2,1)S(1)}, bf16[384,384]{1,0:T(8,128)(2,1)S(1)}, u32[]{:S(2)}, u32[]{:S(2)}) collective-permute-start(bf16[384,384]{1,0:T(8,128)(2,1)S(1)} %constant_dynamic-slice_fusion.6), channel_id=1, source_target_pairs={{0,4},{4,0},{8,12},{12,8},{16,20},{20,16},{24,28},{28,24},{1,5},{5... | collective-permute-start | bytes 884744 | tf_op jit(solution)/shard_map/ppermute | solution.py:342
  503.8 10.3 %collective-permute-start.75 = (bf16[192,384]{1,0:T(8,128)(2,1)S(1)}, bf16[192,384]{1,0:T(8,128)(2,1)S(1)}, u32[]{:S(2)}, u32[]{:S(2)}) collective-permute-start(bf16[192,384]{1,0:T(8,128)(2,1)S(1)} %constant_dynamic-slice_fusion.1), channel_id=1, source_target_pairs={{0,8},{4,12},{8,0},{12,4},{16,24},{20,28},{24,16},{28,20},{1,9},{5... | collective-permute-start | bytes 442376 | tf_op jit(solution)/shard_map/ppermute | solution.py:342
  506.0 10.4 %collective-permute-start.67 = (bf16[192,384]{1,0:T(8,128)(2,1)S(1)}, bf16[192,384]{1,0:T(8,128)(2,1)S(1)}, u32[]{:S(2)}, u32[]{:S(2)}) collective-permute-start(bf16[192,384]{1,0:T(8,128)(2,1)S(1)} %constant_dynamic-slice_fusion.5), channel_id=1, source_target_pairs={{0,8},{4,12},{8,0},{12,4},{16,24},{20,28},{24,16},{28,20},{1,9},{5... | collective-permute-start | bytes 442376 | tf_op jit(solution)/shard_map/ppermute | solution.py:342
  506.1 11.1 %collective-permute-start.58 = (bf16[48,768]{1,0:T(8,128)(2,1)S(1)}, bf16[48,768]{1,0:T(8,128)(2,1)S(1)}, u32[]{:S(2)}, u32[]{:S(2)}) collective-permute-start(bf16[48,768]{1,0:T(8,128)(2,1)S(1)} %constant_dynamic-slice_fusion.8), channel_id=1, source_target_pairs={{0,16},{4,20},{8,24},{12,28},{16,0},{20,4},{24,8},{28,12},{1,17},{... | collective-permute-start | bytes 221192 | tf_op jit(solution)/shard_map/ppermute | solution.py:342
  508.1 11.4 %collective-permute-start.50 = (bf16[48,768]{1,0:T(8,128)(2,1)S(1)}, bf16[48,768]{1,0:T(8,128)(2,1)S(1)}, u32[]{:S(2)}, u32[]{:S(2)}) collective-permute-start(bf16[48,768]{1,0:T(8,128)(2,1)S(1)} %constant_dynamic-slice_fusion.12), channel_id=1, source_target_pairs={{0,16},{4,20},{8,24},{12,28},{16,0},{20,4},{24,8},{28,12},{1,17},{... | collective-permute-start | bytes 221192 | tf_op jit(solution)/shard_map/ppermute | solution.py:342
  514.1 11.1 %collective-permute-start.76 = (bf16[96,384]{1,0:T(8,128)(2,1)S(1)}, bf16[96,384]{1,0:T(8,128)(2,1)S(1)}, u32[]{:S(2)}, u32[]{:S(2)}) collective-permute-start(bf16[96,384]{1,0:T(8,128)(2,1)S(1)} %constant_dynamic-slice_fusion), channel_id=1, source_target_pairs={{0,16},{4,20},{8,24},{12,28},{16,0},{20,4},{24,8},{28,12},{1,17},{... | collective-permute-start | bytes 221192 | tf_op jit(solution)/shard_map/ppermute | solution.py:342
  516.4 10.4 %collective-permute-start.68 = (bf16[96,384]{1,0:T(8,128)(2,1)S(1)}, bf16[96,384]{1,0:T(8,128)(2,1)S(1)}, u32[]{:S(2)}, u32[]{:S(2)}) collective-permute-start(bf16[96,384]{1,0:T(8,128)(2,1)S(1)} %constant_dynamic-slice_fusion.4), channel_id=1, source_target_pairs={{0,16},{4,20},{8,24},{12,28},{16,0},{20,4},{24,8},{28,12},{1,17},{... | collective-permute-start | bytes 221192 | tf_op jit(solution)/shard_map/ppermute | solution.py:342
  517.3 11.1 %collective-permute-start.59 = (bf16[48,768]{1,0:T(8,128)(2,1)S(1)}, bf16[48,768]{1,0:T(8,128)(2,1)S(1)}, u32[]{:S(2)}, u32[]{:S(2)}) collective-permute-start(bf16[48,768]{1,0:T(8,128)(2,1)S(1)} %add_convert_fusion.26), channel_id=1, source_target_pairs={{0,16},{4,20},{8,24},{12,28},{16,0},{20,4},{24,8},{28,12},{1,17},{... | collective-permute-start | bytes 221192 | tf_op jit(solution)/shard_map/ppermute | solution.py:342
  519.5 12.1 %collective-permute-start.51 = (bf16[48,768]{1,0:T(8,128)(2,1)S(1)}, bf16[48,768]{1,0:T(8,128)(2,1)S(1)}, u32[]{:S(2)}, u32[]{:S(2)}) collective-permute-start(bf16[48,768]{1,0:T(8,128)(2,1)S(1)} %add_convert_fusion.27), channel_id=1, source_target_pairs={{0,16},{4,20},{8,24},{12,28},{16,0},{20,4},{24,8},{28,12},{1,17},{... | collective-permute-start | bytes 221192 | tf_op jit(solution)/shard_map/ppermute | solution.py:342
  525.2 8.8 %collective-permute-start.77 = (bf16[96,384]{1,0:T(8,128)(2,1)S(1)}, bf16[96,384]{1,0:T(8,128)(2,1)S(1)}, u32[]{:S(2)}, u32[]{:S(2)}) collective-permute-start(bf16[96,384]{1,0:T(8,128)(2,1)S(1)} %add_convert_fusion.24), channel_id=1, source_target_pairs={{0,16},{4,20},{8,24},{12,28},{16,0},{20,4},{24,8},{28,12},{1,17},{... | collective-permute-start | bytes 221192 | tf_op jit(solution)/shard_map/ppermute | solution.py:342
  528.4 8.8 %collective-permute-start.60 = (bf16[96,768]{1,0:T(8,128)(2,1)S(1)}, bf16[96,768]{1,0:T(8,128)(2,1)S(1)}, u32[]{:S(2)}, u32[]{:S(2)}) collective-permute-start(bf16[96,768]{1,0:T(8,128)(2,1)S(1)} %pad_maximum_fusion.33), channel_id=1, source_target_pairs={{0,8},{4,12},{8,0},{12,4},{16,24},{20,28},{24,16},{28,20},{1,9},{5... | collective-permute-start | bytes 442376 | tf_op jit(solution)/shard_map/ppermute | solution.py:342
  531.7 8.7 %collective-permute-start.52 = (bf16[96,768]{1,0:T(8,128)(2,1)S(1)}, bf16[96,768]{1,0:T(8,128)(2,1)S(1)}, u32[]{:S(2)}, u32[]{:S(2)}) collective-permute-start(bf16[96,768]{1,0:T(8,128)(2,1)S(1)} %pad_maximum_fusion.32), channel_id=1, source_target_pairs={{0,8},{4,12},{8,0},{12,4},{16,24},{20,28},{24,16},{28,20},{1,9},{5... | collective-permute-start | bytes 442376 | tf_op jit(solution)/shard_map/ppermute | solution.py:342
  534.1 9.5 %collective-permute-start.78 = (bf16[192,384]{1,0:T(8,128)(2,1)S(1)}, bf16[192,384]{1,0:T(8,128)(2,1)S(1)}, u32[]{:S(2)}, u32[]{:S(2)}) collective-permute-start(bf16[192,384]{1,0:T(8,128)(2,1)S(1)} %pad_maximum_fusion.35), channel_id=1, source_target_pairs={{0,8},{4,12},{8,0},{12,4},{16,24},{20,28},{24,16},{28,20},{1,9},{5... | collective-permute-start | bytes 442376 | tf_op jit(solution)/shard_map/ppermute | solution.py:342
  534.9 10.8 %collective-permute-start.70 = (bf16[192,384]{1,0:T(8,128)(2,1)S(1)}, bf16[192,384]{1,0:T(8,128)(2,1)S(1)}, u32[]{:S(2)}, u32[]{:S(2)}) collective-permute-start(bf16[192,384]{1,0:T(8,128)(2,1)S(1)} %pad_maximum_fusion.34), channel_id=1, source_target_pairs={{0,8},{4,12},{8,0},{12,4},{16,24},{20,28},{24,16},{28,20},{1,9},{5... | collective-permute-start | bytes 442376 | tf_op jit(solution)/shard_map/ppermute | solution.py:342
  537.3 10.5 %collective-permute-start.61 = (bf16[192,768]{1,0:T(8,128)(2,1)S(1)}, bf16[192,768]{1,0:T(8,128)(2,1)S(1)}, u32[]{:S(2)}, u32[]{:S(2)}) collective-permute-start(bf16[192,768]{1,0:T(8,128)(2,1)S(1)} %pad_maximum_fusion.25), channel_id=1, source_target_pairs={{0,2},{1,3},{2,0},{3,1},{4,6},{5,7},{6,4},{7,5},{8,10},{9,11},{10,... | collective-permute-start | bytes 884744 | tf_op jit(solution)/shard_map/ppermute | solution.py:342
  545.8 10.0 %collective-permute-start.71 = (bf16[384,384]{1,0:T(8,128)(2,1)S(1)}, bf16[384,384]{1,0:T(8,128)(2,1)S(1)}, u32[]{:S(2)}, u32[]{:S(2)}) collective-permute-start(bf16[384,384]{1,0:T(8,128)(2,1)S(1)} %pad_maximum_fusion.26), channel_id=1, source_target_pairs={{0,4},{4,0},{8,12},{12,8},{16,20},{20,16},{24,28},{28,24},{1,5},{5... | collective-permute-start | bytes 884744 | tf_op jit(solution)/shard_map/ppermute | solution.py:342
  548.0 20.5 %collective-permute-start.62 = (bf16[384,768]{1,0:T(8,128)(2,1)S(1)}, bf16[384,768]{1,0:T(8,128)(2,1)S(1)}, u32[]{:S(2)}, u32[]{:S(2)}) collective-permute-start(bf16[384,768]{1,0:T(8,128)(2,1)S(1)} %pad_maximum_fusion.17), channel_id=1, source_target_pairs={{0,4},{4,0},{8,12},{12,8},{16,20},{20,16},{24,28},{28,24},{1,5},{5... | collective-permute-start | bytes 1769480 | tf_op jit(solution)/shard_map/ppermute | solution.py:342
  548.3 20.4 %collective-permute-start.54 = (bf16[384,768]{1,0:T(8,128)(2,1)S(1)}, bf16[384,768]{1,0:T(8,128)(2,1)S(1)}, u32[]{:S(2)}, u32[]{:S(2)}) collective-permute-start(bf16[384,768]{1,0:T(8,128)(2,1)S(1)} %pad_maximum_fusion.16), channel_id=1, source_target_pairs={{0,2},{1,3},{2,0},{3,1},{4,6},{5,7},{6,4},{7,5},{8,10},{9,11},{10,... | collective-permute-start | bytes 1769480 | tf_op jit(solution)/shard_map/ppermute | solution.py:342
  552.1 27.1 %collective-permute-start.80 = (bf16[768,384]{1,0:T(8,128)(2,1)S(1)}, bf16[768,384]{1,0:T(8,128)(2,1)S(1)}, u32[]{:S(2)}, u32[]{:S(2)}) collective-permute-start(bf16[768,384]{1,0:T(8,128)(2,1)S(1)} %pad_maximum_fusion.19), channel_id=1, source_target_pairs={{0,4},{4,0},{8,12},{12,8},{16,20},{20,16},{24,28},{28,24},{1,5},{5... | collective-permute-start | bytes 1769480 | tf_op jit(solution)/shard_map/ppermute | solution.py:342
  556.0 23.4 %collective-permute-start.72 = (bf16[768,384]{1,0:T(8,128)(2,1)S(1)}, bf16[768,384]{1,0:T(8,128)(2,1)S(1)}, u32[]{:S(2)}, u32[]{:S(2)}) collective-permute-start(bf16[768,384]{1,0:T(8,128)(2,1)S(1)} %pad_maximum_fusion.18), channel_id=1, source_target_pairs={{0,2},{1,3},{2,0},{3,1},{4,6},{5,7},{6,4},{7,5},{8,10},{9,11},{10,... | collective-permute-start | bytes 1769480 | tf_op jit(solution)/shard_map/ppermute | solution.py:342
  569.1 18.1 %collective-permute-start.63 = (bf16[768,1536]{1,0:T(8,128)(2,1)S(1)}, bf16[768,1536]{1,0:T(8,128)(2,1)S(1)}, u32[]{:S(2)}, u32[]{:S(2)}) collective-permute-start(bf16[768,1536]{1,0:T(8,128)(2,1)S(1)} %maximum_maximum_fusion), channel_id=1, source_target_pairs={{0,1},{1,0},{2,3},{3,2},{4,5},{5,4},{6,7},{7,6},{8,9},{9,8},{10,11... | collective-permute-start | bytes 7077896 | tf_op jit(solution)/shard_map/ppermute | solution.py:342
  579.9 22.6 %collective-permute-start.81 = (bf16[1536,768]{1,0:T(8,128)(2,1)S(1)}, bf16[1536,768]{1,0:T(8,128)(2,1)S(1)}, u32[]{:S(2)}, u32[]{:S(2)}) collective-permute-start(bf16[1536,768]{1,0:T(8,128)(2,1)S(1)} %maximum_maximum_fusion.1), channel_id=1, source_target_pairs={{0,1},{1,0},{2,3},{3,2},{4,5},{5,4},{6,7},{7,6},{8,9},{9,8},{10,11... | collective-permute-start | bytes 7077896 | tf_op jit(solution)/shard_map/ppermute | solution.py:342
  (86 other events, 587.4 us)
